TPU v7x, 32 devices: a whole 2x2x4 slice. The times are simulated.
32 devices in a mesh: section: 4 (over y, x), dp: 4 (over z), mp: 2 (over core).
Axes of the slice: x: 2, y: 2, z: 4, core: 2. Of those that a mesh axis runs over, the one named last changes fastest.
Arguments:
- activations: bfloat16 [4, 3, 768, 2048], P('section', None, 'dp'), may hold values from -6 to 6
- out_grad: bfloat16 [3, 768, 2048], P(None, 'dp'), may hold values from -6 to 6
- weight_in: bfloat16 [4, 2048, 4096], P('section', 'dp', 'mp'), may hold values from -0.125 to 0.125
- weight_out: bfloat16 [4, 4096, 2048], P('section', 'mp', 'dp'), may hold values from -0.09375 to 0.09375
- lengths: int32 [3, 4], P(None, 'dp'), may hold values from 48 to 192, as said below
Outputs:
- input_grads: bfloat16 [4, 3, 768, 2048], P('section', None, 'dp', 'mp')
- grad_weight_in: bfloat16 [4, 2048, 4096], P('section', 'dp', 'mp')
- grad_weight_out: bfloat16 [4, 4096, 2048], P('section', 'mp', 'dp')
Inputs may be any that keep to these rules, and one draw needn't show every extreme that they name: `lengths`: some replica holds a full micro-batch of 192 live tokens in every draw.
All inputs are finite; a program needn't handle non-finite values.
Results may differ from a plain program's by a relative error of at most 0.0095.
Values may be sent and summed in bfloat16 or wider, within the bound.
A program may use at most 192 MiB of HBM per device.

v0:
```python
import jax
import jax.numpy as jnp
from jax import lax
from jax.sharding import PartitionSpec as P


def passed_along(x, axis, by):
    devices = lax.axis_size(axis)
    pairs = [(i, i + by) for i in range(devices) if 0 <= i + by < devices]
    return lax.ppermute(x, axis, pairs)


def cross(left, right):
    return lax.dot_general(
        left, right, (((0,), (0,)), ((), ())), preferred_element_type=jnp.float32
    )


def times_transposed(left, right):
    return lax.dot_general(
        left, right, (((1,), (1,)), ((), ())), preferred_element_type=jnp.float32
    )


def local(activations, out_grad, weight_in, weight_out, lengths):
    sections = lax.axis_size("section")
    section_index = lax.axis_index("section")
    mp_count = lax.axis_size("mp")
    mp_index = lax.axis_index("mp")
    micro_count, row_count, width = out_grad.shape
    slice_width = width // mp_count
    hidden_width = weight_in.shape[2]
    full_in, full_out = (
        lax.all_gather(weight_in[0], "dp", axis=0, tiled=True),
        lax.all_gather(weight_out[0], "dp", axis=1, tiled=True),
    )
    valid = jnp.arange(row_count)[None, :] < lengths
    masked = jnp.where(valid[..., None], out_grad, jnp.zeros_like(out_grad))
    masked_slice = lax.dynamic_slice_in_dim(masked, mp_index * slice_width, slice_width, 2)
    saved_inputs = activations[0]

    def backward_pass(operands):
        x_now, grad_full = operands
        pre = jnp.dot(x_now, full_in, preferred_element_type=jnp.float32)
        sigma = jax.nn.sigmoid(pre)
        act = (pre * sigma).astype(jnp.bfloat16)
        grad_act = times_transposed(grad_full, full_out)
        dpre = (grad_act * sigma * (1.0 + pre * (1.0 - sigma))).astype(jnp.bfloat16)
        partial_sum = times_transposed(dpre, full_in)
        return (act, dpre, partial_sum)

    def resting(operands):
        empty = jnp.zeros((row_count, hidden_width), jnp.bfloat16)
        return (empty, empty, jnp.zeros((row_count, width), jnp.float32))

    def chain_step(clock, carry):
        incoming, grads, grad_store, act_store, dh_store = carry
        micro_index = clock - (sections - 1 - section_index)
        active = (micro_index >= 0) & (micro_index < micro_count)
        micro_slot = jnp.clip(micro_index, 0, micro_count - 1)
        first = lax.dynamic_index_in_dim(masked_slice, micro_slot, 0, keepdims=False)
        own_slice = jnp.where(section_index == sections - 1, first, incoming)
        grad_full = lax.all_gather(own_slice, "mp", axis=1, tiled=True)
        x_now = lax.dynamic_index_in_dim(saved_inputs, micro_slot, 0, keepdims=False)
        act, dpre, partial_sum = lax.cond(active, backward_pass, resting, (x_now, grad_full))
        reduced = lax.psum_scatter(partial_sum, "mp", scatter_dimension=1, tiled=True)
        result = (own_slice.astype(jnp.float32) + reduced).astype(jnp.bfloat16)
        grads = jnp.where(
            active, lax.dynamic_update_index_in_dim(grads, result, micro_slot, 0), grads
        )
        grad_store = jnp.where(
            active,
            lax.dynamic_update_index_in_dim(grad_store, grad_full, micro_slot, 0),
            grad_store,
        )
        act_store = jnp.where(
            active, lax.dynamic_update_index_in_dim(act_store, act, micro_slot, 0), act_store
        )
        dh_store = jnp.where(
            active, lax.dynamic_update_index_in_dim(dh_store, dpre, micro_slot, 0), dh_store
        )
        sent = passed_along(result, "section", -1)
        return (sent, grads, grad_store, act_store, dh_store)

    start = (
        jnp.zeros((row_count, slice_width), jnp.bfloat16),
        jnp.zeros((micro_count, row_count, slice_width), jnp.bfloat16),
        jnp.zeros((micro_count, row_count, width), jnp.bfloat16),
        jnp.zeros((micro_count, row_count, hidden_width), jnp.bfloat16),
        jnp.zeros((micro_count, row_count, hidden_width), jnp.bfloat16),
    )
    final = lax.fori_loop(0, sections + micro_count - 1, chain_step, start)
    grads = final[1]
    grad_flat = final[2].reshape(-1, width)
    act_flat = final[3].reshape(-1, hidden_width)
    dh_flat = final[4].reshape(-1, hidden_width)
    input_flat = saved_inputs.reshape(-1, width)
    dw_in, dw_out = (
        lax.psum_scatter(cross(input_flat, dh_flat), "dp", scatter_dimension=0, tiled=True),
        lax.psum_scatter(cross(act_flat, grad_flat), "dp", scatter_dimension=1, tiled=True),
    )
    return (grads[None], dw_in.astype(jnp.bfloat16)[None], dw_out.astype(jnp.bfloat16)[None])


def solution(mesh):
    return jax.shard_map(
        local,
        mesh=mesh,
        in_specs=(
            P("section", None, "dp", None),
            P(None, "dp", None),
            P("section", "dp", "mp"),
            P("section", "mp", "dp"),
            P(None, "dp"),
        ),
        out_specs=(
            P("section", None, "dp", "mp"),
            P("section", "dp", "mp"),
            P("section", "mp", "dp"),
        ),
        check_vma=False,
    )
```

profile of v0, /device:TPU:0, one launch (start us, length us, event | category | flops | bytes accessed | tf_op | source)
XLA Modules:
  0.0 1165.0 jit_solution(14669834138763346836)
XLA Ops:
  10.1 151.8 %all-gather.7.cloned.1.call-done = bf16[1,2048,2048]{2,1,0:T(8,128)(2,1)} async-done(((bf16[1,512,2048]{2,1,0:T(8,128)(2,1)}), bf16[1,2048,2048]{2,1,0:T(8,128)(2,1)}) %all-gather.7.cloned.1.call-update) | async-done | bytes 8388624 | tf_op jit(solution)/shard_map/all_gather | solution.py:34
  162.0 149.5 %all-gather.5.cloned.1.call-done = bf16[1,2048,2048]{2,1,0:T(8,128)(2,1)} async-done(((bf16[1,2048,512]{2,1,0:T(8,128)(2,1)}), bf16[1,2048,2048]{2,1,0:T(8,128)(2,1)}) %all-gather.5.cloned.1.call-update) | async-done | bytes 8388624 | tf_op jit(solution)/shard_map/all_gather | solution.py:35
  312.6 1.7 broadcast.47.clone.1
  316.0 1.7 broadcast.47
  317.8 259.2 %while.23 = (s32[]{:T(128)}, bf16[192,1024]{1,0:T(8,128)(2,1)S(1)}, bf16[3,192,1024]{2,1,0:T(8,128)(2,1)}, bf16[3,192,2048]{2,1,0:T(8,128)(2,1)}, bf16[3,192,204...) while((s32[]{:T(128)}, bf16[192,1024]{1,0:T(8,128)(2,1)S(1)}, ...), condition=%wide.region_4.5_spmd, body=%wide.region_0.4_spmd.sunk | while | flops 4839505920 | bytes 149161552 | solution.py:92
  318.8 2.4 all_gather.18
  323.6 3.3 fusion.22
  326.9 17.3 %reduce-scatter.8.cloned.1.call-done = f32[192,1024]{1,0:T(8,128)} async-done(((f32[192,2048]{1,0:T(8,128)}), f32[192,1024]{1,0:T(8,128)}) %reduce-scatter.8.cloned.1.call-update) | async-done | bytes 786448 | tf_op jit(solution)/shard_map/while/body/eval_jaxpr/reduce_scatter | solution.py:66
  347.3 11.6 collective-permute-done
  360.0 2.4 all_gather.18
  364.8 3.3 fusion.22
  368.0 19.4 %reduce-scatter.8.cloned.1.call-done = f32[192,1024]{1,0:T(8,128)} async-done(((f32[192,2048]{1,0:T(8,128)}), f32[192,1024]{1,0:T(8,128)}) %reduce-scatter.8.cloned.1.call-update) | async-done | bytes 786448 | tf_op jit(solution)/shard_map/while/body/eval_jaxpr/reduce_scatter | solution.py:66
  390.6 11.6 collective-permute-done
  403.2 2.4 all_gather.18
  408.0 3.3 fusion.22
  411.3 20.3 %reduce-scatter.8.cloned.1.call-done = f32[192,1024]{1,0:T(8,128)} async-done(((f32[192,2048]{1,0:T(8,128)}), f32[192,1024]{1,0:T(8,128)}) %reduce-scatter.8.cloned.1.call-update) | async-done | bytes 786448 | tf_op jit(solution)/shard_map/while/body/eval_jaxpr/reduce_scatter | solution.py:66
  434.7 11.6 collective-permute-done
  447.4 2.4 all_gather.18
  449.7 14.4 %conditional.2 = (f32[192,2048]{1,0:T(8,128)S(1)}, bf16[1,192,2048]{2,1,0:T(8,128)(2,1)S(1)}, bf16[1,192,2048]{2,1,0:T(8,128)(2,1)}) conditional(s32[]{:T(128)} %convert_element_type.54, () %tuple.62, (bf16[192,2048]{1,0:T(8,128)(2,1)S(1)}, bf16[2048,2048]{1,0:T(8,128)(2,1)}, bf16[3,192,2048]{2,1,0:T(8,128)(2,1)}, s32[]{:T(128)}, ...), branch_computations={%region_1.1_spmd, %region_2.2_spmd} | conditional | flops 4837343232 | bytes 94110304 | solution.py:65
  449.7 5.6 fusion.2
  455.8 4.0 fusion.1
  459.7 4.0 fusion.9
  465.4 3.5 fusion.22
  468.9 6.9 reduce-scatter.8.cloned.1.call-done
  478.9 11.6 collective-permute-done
  491.5 2.4 all_gather.18
  493.9 14.4 %conditional.2 = (f32[192,2048]{1,0:T(8,128)S(1)}, bf16[1,192,2048]{2,1,0:T(8,128)(2,1)S(1)}, bf16[1,192,2048]{2,1,0:T(8,128)(2,1)}) conditional(s32[]{:T(128)} %convert_element_type.54, () %tuple.62, (bf16[192,2048]{1,0:T(8,128)(2,1)S(1)}, bf16[2048,2048]{1,0:T(8,128)(2,1)}, bf16[3,192,2048]{2,1,0:T(8,128)(2,1)}, s32[]{:T(128)}, ...), branch_computations={%region_1.1_spmd, %region_2.2_spmd} | conditional | flops 4837343232 | bytes 94110304 | solution.py:65
  493.9 5.6 fusion.2
  499.9 4.0 fusion.1
  503.9 4.0 fusion.9
  509.5 3.5 fusion.22
  513.0 6.9 reduce-scatter.8.cloned.1.call-done
  523.0 11.6 collective-permute-done
  535.7 2.4 all_gather.18
  538.0 14.4 %conditional.2 = (f32[192,2048]{1,0:T(8,128)S(1)}, bf16[1,192,2048]{2,1,0:T(8,128)(2,1)S(1)}, bf16[1,192,2048]{2,1,0:T(8,128)(2,1)}) conditional(s32[]{:T(128)} %convert_element_type.54, () %tuple.62, (bf16[192,2048]{1,0:T(8,128)(2,1)S(1)}, bf16[2048,2048]{1,0:T(8,128)(2,1)}, bf16[3,192,2048]{2,1,0:T(8,128)(2,1)}, s32[]{:T(128)}, ...), branch_computations={%region_1.1_spmd, %region_2.2_spmd} | conditional | flops 4837343232 | bytes 94110304 | solution.py:65
  538.0 5.6 fusion.2
  544.0 4.0 fusion.1
  548.0 4.0 fusion.9
  553.7 3.5 fusion.22
  557.2 5.0 reduce-scatter.8.cloned.1.call-done
  565.3 11.6 collective-permute-done
  577.1 12.2 %convolution_bitcast_fusion.1 = f32[2048,2048]{0,1:T(8,128)} fusion(bf16[576,2048]{1,0:T(8,128)(2,1)} %bitcast.46, bf16[576,2048]{1,0:T(8,128)(2,1)} %bitcast.53), kind=kOutput, calls=%fused_computation.19 | convolution fusion | flops 4831838208 | bytes 21495808 | tf_op jit(solution)/shard_map/dot_general | solution.py:14
  591.0 11.8 %convolution_bitcast_fusion = f32[2048,2048]{1,0:T(8,128)} fusion(bf16[3,192,2048]{2,1,0:T(8,128)(2,1)} %get-tuple-element.302, bf16[3,192,2048]{2,1,0:T(8,128)(2,1)S(1)} %copy-done.1), kind=kOutput, calls=%fused_computation.18 | convolution fusion | flops 4831838208 | bytes 21495808 | tf_op jit(solution)/shard_map/dot_general | solution.py:14
  602.8 268.2 %reduce-scatter.4.cloned.1.call-done = f32[512,2048]{0,1:T(8,128)} async-done(((f32[2048,2048]{0,1:T(8,128)}), f32[512,2048]{0,1:T(8,128)}) %reduce-scatter.4.cloned.1.call-update) | async-done | bytes 4194320 | tf_op jit(solution)/shard_map/reduce_scatter | solution.py:99
  871.0 2.5 convert_bitcast_fusion.1
  873.5 2.4 copy.8
  875.9 278.5 %reduce-scatter.6.cloned.1.call-done = f32[2048,512]{1,0:T(8,128)} async-done(((f32[2048,2048]{1,0:T(8,128)}), f32[2048,512]{1,0:T(8,128)}) %reduce-scatter.6.cloned.1.call-update) | async-done | bytes 4194320 | tf_op jit(solution)/shard_map/reduce_scatter | solution.py:100
  1154.4 3.8 convert_bitcast_fusion
  (151 shorter events, 49.3 us)
Async XLA Ops:
  7.2 154.8 %all-gather.7.cloned.1.call-start = ((), (), s32[]{:S(2)}) async-start(), calls=%async_computation.6 | async-start | bytes 10485760 | tf_op jit(solution)/shard_map/all_gather | solution.py:34
  7.9 303.5 %all-gather.5.cloned.1.call-start = ((), (), s32[]{:S(2)}) async-start(), calls=%async_computation.5 | async-start | bytes 10485760 | tf_op jit(solution)/shard_map/all_gather | solution.py:35
  317.8 26.4 %reduce-scatter.8.cloned.1.call-start = ((), (), s32[]{:S(2)}) async-start(), calls=%async_computation.7 | async-start | bytes 2359296 | tf_op jit(solution)/shard_map/while/body/eval_jaxpr/reduce_scatter | solution.py:66
  323.6 20.6 %copy-start.4 = (bf16[3,192,1024]{2,1,0:T(8,128)(2,1)S(1)}, bf16[3,192,1024]{2,1,0:T(8,128)(2,1)}, u32[]{:S(2)}) copy-start(bf16[3,192,1024]{2,1,0:T(8,128)(2,1)} %get-tuple-element.446) | copy-start | bytes 3538948 | tf_op jit(solution)/shard_map/while
  344.2 2.8 copy-start.2
  345.7 13.2 %copy-start.5 = (bf16[3,192,1024]{2,1,0:T(8,128)(2,1)}, bf16[3,192,1024]{2,1,0:T(8,128)(2,1)S(1)}, u32[]{:S(2)}) copy-start(bf16[3,192,1024]{2,1,0:T(8,128)(2,1)S(1)} %get-tuple-element.462) | copy-start | bytes 3538948 | tf_op jit(solution)/shard_map/while
  345.7 13.2 %collective-permute-start = (bf16[192,1024]{1,0:T(8,128)(2,1)S(1)}, bf16[192,1024]{1,0:T(8,128)(2,1)S(1)}, u32[]{:S(2)}, u32[]{:S(2)}) collective-permute-start(bf16[192,1024]{1,0:T(8,128)(2,1)S(1)} %get-tuple-element.416), channel_id=1, source_target_pairs={{8,0},{16,8},{24,16},{9,1},{17,9},{25,17},{10,2},{18,10},{26,18},{... | collective-permute-start | bytes 1179656 | tf_op jit(solution)/shard_map/while/body/eval_jaxpr/ppermute | solution.py:10
  347.3 11.6 copy-start.3
  358.9 28.5 %reduce-scatter.8.cloned.1.call-start = ((), (), s32[]{:S(2)}) async-start(), calls=%async_computation.7 | async-start | bytes 2359296 | tf_op jit(solution)/shard_map/while/body/eval_jaxpr/reduce_scatter | solution.py:66
  364.8 22.7 %copy-start.4 = (bf16[3,192,1024]{2,1,0:T(8,128)(2,1)S(1)}, bf16[3,192,1024]{2,1,0:T(8,128)(2,1)}, u32[]{:S(2)}) copy-start(bf16[3,192,1024]{2,1,0:T(8,128)(2,1)} %get-tuple-element.446) | copy-start | bytes 3538948 | tf_op jit(solution)/shard_map/while
  387.4 2.8 copy-start.2
  388.9 13.2 %copy-start.5 = (bf16[3,192,1024]{2,1,0:T(8,128)(2,1)}, bf16[3,192,1024]{2,1,0:T(8,128)(2,1)S(1)}, u32[]{:S(2)}) copy-start(bf16[3,192,1024]{2,1,0:T(8,128)(2,1)S(1)} %get-tuple-element.462) | copy-start | bytes 3538948 | tf_op jit(solution)/shard_map/while
  389.0 13.2 %collective-permute-start = (bf16[192,1024]{1,0:T(8,128)(2,1)S(1)}, bf16[192,1024]{1,0:T(8,128)(2,1)S(1)}, u32[]{:S(2)}, u32[]{:S(2)}) collective-permute-start(bf16[192,1024]{1,0:T(8,128)(2,1)S(1)} %get-tuple-element.416), channel_id=1, source_target_pairs={{8,0},{16,8},{24,16},{9,1},{17,9},{25,17},{10,2},{18,10},{26,18},{... | collective-permute-start | bytes 1179656 | tf_op jit(solution)/shard_map/while/body/eval_jaxpr/ppermute | solution.py:10
  390.6 11.6 copy-start.3
  402.2 29.4 %reduce-scatter.8.cloned.1.call-start = ((), (), s32[]{:S(2)}) async-start(), calls=%async_computation.7 | async-start | bytes 2359296 | tf_op jit(solution)/shard_map/while/body/eval_jaxpr/reduce_scatter | solution.py:66
  408.0 23.6 %copy-start.4 = (bf16[3,192,1024]{2,1,0:T(8,128)(2,1)S(1)}, bf16[3,192,1024]{2,1,0:T(8,128)(2,1)}, u32[]{:S(2)}) copy-start(bf16[3,192,1024]{2,1,0:T(8,128)(2,1)} %get-tuple-element.446) | copy-start | bytes 3538948 | tf_op jit(solution)/shard_map/while
  431.6 2.8 copy-start.2
  433.1 13.2 %copy-start.5 = (bf16[3,192,1024]{2,1,0:T(8,128)(2,1)}, bf16[3,192,1024]{2,1,0:T(8,128)(2,1)S(1)}, u32[]{:S(2)}) copy-start(bf16[3,192,1024]{2,1,0:T(8,128)(2,1)S(1)} %get-tuple-element.462) | copy-start | bytes 3538948 | tf_op jit(solution)/shard_map/while
  433.1 13.2 %collective-permute-start = (bf16[192,1024]{1,0:T(8,128)(2,1)S(1)}, bf16[192,1024]{1,0:T(8,128)(2,1)S(1)}, u32[]{:S(2)}, u32[]{:S(2)}) collective-permute-start(bf16[192,1024]{1,0:T(8,128)(2,1)S(1)} %get-tuple-element.416), channel_id=1, source_target_pairs={{8,0},{16,8},{24,16},{9,1},{17,9},{25,17},{10,2},{18,10},{26,18},{... | collective-permute-start | bytes 1179656 | tf_op jit(solution)/shard_map/while/body/eval_jaxpr/ppermute | solution.py:10
  434.7 11.6 copy-start.3
  446.3 29.4 %reduce-scatter.8.cloned.1.call-start = ((), (), s32[]{:S(2)}) async-start(), calls=%async_computation.7 | async-start | bytes 2359296 | tf_op jit(solution)/shard_map/while/body/eval_jaxpr/reduce_scatter | solution.py:66
  449.7 6.0 copy-start.7
  449.7 10.0 slice-start
  455.7 4.0 slice-start.1
  465.4 10.4 copy-start.4
  475.7 2.8 copy-start.2
  477.2 13.2 %copy-start.5 = (bf16[3,192,1024]{2,1,0:T(8,128)(2,1)}, bf16[3,192,1024]{2,1,0:T(8,128)(2,1)S(1)}, u32[]{:S(2)}) copy-start(bf16[3,192,1024]{2,1,0:T(8,128)(2,1)S(1)} %get-tuple-element.462) | copy-start | bytes 3538948 | tf_op jit(solution)/shard_map/while
  477.2 13.2 %collective-permute-start = (bf16[192,1024]{1,0:T(8,128)(2,1)S(1)}, bf16[192,1024]{1,0:T(8,128)(2,1)S(1)}, u32[]{:S(2)}, u32[]{:S(2)}) collective-permute-start(bf16[192,1024]{1,0:T(8,128)(2,1)S(1)} %get-tuple-element.416), channel_id=1, source_target_pairs={{8,0},{16,8},{24,16},{9,1},{17,9},{25,17},{10,2},{18,10},{26,18},{... | collective-permute-start | bytes 1179656 | tf_op jit(solution)/shard_map/while/body/eval_jaxpr/ppermute | solution.py:10
  478.8 11.6 copy-start.3
  490.4 29.4 %reduce-scatter.8.cloned.1.call-start = ((), (), s32[]{:S(2)}) async-start(), calls=%async_computation.7 | async-start | bytes 2359296 | tf_op jit(solution)/shard_map/while/body/eval_jaxpr/reduce_scatter | solution.py:66
  493.9 6.0 copy-start.7
  493.9 10.0 slice-start
  499.9 4.0 slice-start.1
  509.5 10.4 copy-start.4
  521.4 13.2 %copy-start.5 = (bf16[3,192,1024]{2,1,0:T(8,128)(2,1)}, bf16[3,192,1024]{2,1,0:T(8,128)(2,1)S(1)}, u32[]{:S(2)}) copy-start(bf16[3,192,1024]{2,1,0:T(8,128)(2,1)S(1)} %get-tuple-element.462) | copy-start | bytes 3538948 | tf_op jit(solution)/shard_map/while
  521.4 13.2 %collective-permute-start = (bf16[192,1024]{1,0:T(8,128)(2,1)S(1)}, bf16[192,1024]{1,0:T(8,128)(2,1)S(1)}, u32[]{:S(2)}, u32[]{:S(2)}) collective-permute-start(bf16[192,1024]{1,0:T(8,128)(2,1)S(1)} %get-tuple-element.416), channel_id=1, source_target_pairs={{8,0},{16,8},{24,16},{9,1},{17,9},{25,17},{10,2},{18,10},{26,18},{... | collective-permute-start | bytes 1179656 | tf_op jit(solution)/shard_map/while/body/eval_jaxpr/ppermute | solution.py:10
  523.0 11.6 copy-start.3
  534.6 27.6 %reduce-scatter.8.cloned.1.call-start = ((), (), s32[]{:S(2)}) async-start(), calls=%async_computation.7 | async-start | bytes 2359296 | tf_op jit(solution)/shard_map/while/body/eval_jaxpr/reduce_scatter | solution.py:66
  538.0 6.0 copy-start.7
  538.0 10.0 slice-start
  544.0 4.0 slice-start.1
  553.7 8.5 copy-start.4
  562.2 2.8 copy-start.2
  563.7 13.2 %copy-start.5 = (bf16[3,192,1024]{2,1,0:T(8,128)(2,1)}, bf16[3,192,1024]{2,1,0:T(8,128)(2,1)S(1)}, u32[]{:S(2)}) copy-start(bf16[3,192,1024]{2,1,0:T(8,128)(2,1)S(1)} %get-tuple-element.462) | copy-start | bytes 3538948 | tf_op jit(solution)/shard_map/while
  563.7 13.2 %collective-permute-start = (bf16[192,1024]{1,0:T(8,128)(2,1)S(1)}, bf16[192,1024]{1,0:T(8,128)(2,1)S(1)}, u32[]{:S(2)}, u32[]{:S(2)}) collective-permute-start(bf16[192,1024]{1,0:T(8,128)(2,1)S(1)} %get-tuple-element.416), channel_id=1, source_target_pairs={{8,0},{16,8},{24,16},{9,1},{17,9},{25,17},{10,2},{18,10},{26,18},{... | collective-permute-start | bytes 1179656 | tf_op jit(solution)/shard_map/while/body/eval_jaxpr/ppermute | solution.py:10
  565.3 11.6 copy-start.3
  576.9 294.1 %reduce-scatter.4.cloned.1.call-start = ((), (), s32[]{:S(2)}) async-start(), calls=%async_computation.3 | async-start | bytes 20971520 | tf_op jit(solution)/shard_map/reduce_scatter | solution.py:99
  589.4 565.0 %reduce-scatter.6.cloned.1.call-start = ((), (), s32[]{:S(2)}) async-start(), calls=%async_computation.4 | async-start | bytes 20971520 | tf_op jit(solution)/shard_map/reduce_scatter | solution.py:100
  (10 other events, 14.5 us)
Sparse Core Ops, SparseCore 0:
  9.6 152.3 all-gather.6
  163.5 147.8 all-gather.4
  323.7 20.4 reduce-scatter.7
  364.9 22.5 reduce-scatter.7
  408.1 23.4 reduce-scatter.7
  465.5 10.1 reduce-scatter.7
  509.6 10.2 reduce-scatter.7
  553.8 8.3 reduce-scatter.7
  589.5 281.4 reduce-scatter.3
  873.3 281.0 reduce-scatter.5
where the time goes:
time: 1170 us
  waiting for transfers between devices  995 us (85%)
  matrix products  64.7 us (6%)
  other arithmetic  46 us (4%)
  local copies, waits for them, and re-layouts  22.3 us (2%)
  blocking collectives  14.2 us (1%)
  between operations  14.1 us (1%)
    reduce_scatter x1, waiting for transfers between devices, local(): lax.psum_scatter(cross(act_flat, grad_flat), 'dp', scatter_dimension=1, t...  279 us
    reduce_scatter x1, waiting for transfers between devices, local(): lax.psum_scatter(cross(input_flat, dh_flat), 'dp', scatter_dimension=0, t...  268 us
    all_gather x1, waiting for transfers between devices, local(): lax.all_gather(weight_in[0], 'dp', axis=0, tiled=True)  152 us
    all_gather x1, waiting for transfers between devices, local(): lax.all_gather(weight_out[0], 'dp', axis=1, tiled=True)  149 us
    reduce_scatter x6, waiting for transfers between devices, chain_step(): lax.psum_scatter(partial_sum, 'mp', scatter_dimension=1, tiled=True)  75.8 us
    ppermute x6, waiting for transfers between devices, passed_along(): return lax.ppermute(x, axis, pairs)  69.5 us
    dot_general x2, matrix products, cross(): lax.dot_general(left, right, (((0,), (0,)), ((), ())), preferred_element_...  24 us
    dot_general x6, matrix products, times_transposed(): lax.dot_general(left, right, (((1,), (1,)), ((), ())), preferred_element_...  24 us
  transfers between devices with their start and end apart: 16, of which 16 were waited for; matrix products, arithmetic and copies ran while one was open for 3% of the time, Pallas kernels for 0%

commit v1 on v0

v1 whole, which is shorter than its diff:
```python
import jax
import jax.numpy as jnp
from jax import lax
from jax.sharding import PartitionSpec as P


def passed_along(x, axis, by):
    devices = lax.axis_size(axis)
    pairs = [(i, i + by) for i in range(devices) if 0 <= i + by < devices]
    return lax.ppermute(x, axis, pairs)


def swapped(x):
    return lax.ppermute(x, "mp", [(0, 1), (1, 0)])


def cross(left, right):
    return lax.dot_general(
        left, right, (((0,), (0,)), ((), ())), preferred_element_type=jnp.float32
    )


def times_transposed(left, right):
    return lax.dot_general(
        left, right, (((1,), (1,)), ((), ())), preferred_element_type=jnp.float32
    )


def both_halves(x):
    other = swapped(x)
    first = lax.axis_index("mp") == 0
    return jnp.concatenate([jnp.where(first, x, other), jnp.where(first, other, x)], axis=-1)


def slope(pre):
    sigma = jax.nn.sigmoid(pre)
    return sigma * (1.0 + pre * (1.0 - sigma))


def local(activations, out_grad, weight_in, weight_out, lengths):
    sections = lax.axis_size("section")
    section_index = lax.axis_index("section")
    mp_count = lax.axis_size("mp")
    mp_index = lax.axis_index("mp")
    dp_count = lax.axis_size("dp")
    dp_index = lax.axis_index("dp")
    micro_count, row_count, width = out_grad.shape
    half = width // mp_count
    part = weight_in.shape[1]
    hidden = weight_in.shape[2]
    saved = activations[0]
    full_in = lax.all_gather(weight_in[0], "dp", axis=0, tiled=True)
    full_out = lax.all_gather(weight_out[0], "dp", axis=1, tiled=True)
    valid = jnp.arange(row_count)[None, :] < lengths
    own_grad = lax.dynamic_slice_in_dim(out_grad, mp_index * half, half, 2)
    own_grad = jnp.where(valid[..., None], own_grad, jnp.zeros_like(own_grad))
    own_saved = lax.dynamic_slice_in_dim(saved, mp_index * half, half, 2)
    pre = jnp.dot(saved.reshape(-1, width), full_in, preferred_element_type=jnp.float32)
    slopes = slope(pre).reshape(micro_count, row_count, hidden)

    incoming = jnp.zeros((row_count, half), jnp.bfloat16)
    grads = jnp.zeros((micro_count, row_count, half), jnp.bfloat16)
    arrived = jnp.zeros((micro_count, row_count, half), jnp.bfloat16)
    for clock in range(sections + micro_count - 1):
        micro = clock - (sections - 1 - section_index)
        active = (micro >= 0) & (micro < micro_count)
        slot = jnp.clip(micro, 0, micro_count - 1)
        first = lax.dynamic_index_in_dim(own_grad, slot, 0, keepdims=False)
        own = jnp.where(section_index == sections - 1, first, incoming)
        grad_act = times_transposed(both_halves(own), full_out)
        scale = lax.dynamic_index_in_dim(slopes, slot, 0, keepdims=False)
        dpre = (grad_act * scale).astype(jnp.bfloat16)
        terms = times_transposed(dpre, full_in)
        mine = lax.dynamic_slice_in_dim(terms, mp_index * half, half, 1)
        theirs = lax.dynamic_slice_in_dim(terms, (1 - mp_index) * half, half, 1)
        result = own.astype(jnp.float32) + (
            mine + swapped(theirs.astype(jnp.bfloat16)).astype(jnp.float32)
        )
        result = result.astype(jnp.bfloat16)
        if clock < sections + micro_count - 2:
            incoming = passed_along(result, "section", -1)
        grads = jnp.where(active, lax.dynamic_update_index_in_dim(grads, result, slot, 0), grads)
        arrived = jnp.where(active, lax.dynamic_update_index_in_dim(arrived, own, slot, 0), arrived)

    all_saved = lax.all_gather(own_saved, "dp", axis=0, tiled=True)
    all_saved = all_saved.reshape(-1, row_count, half)
    all_grad = lax.all_gather(arrived, "dp", axis=0, tiled=True)
    all_grad = all_grad.reshape(-1, row_count, half)

    chunk = min(4, dp_count)
    steps = micro_count * dp_count // chunk
    rows = chunk * row_count
    total_in = jnp.zeros((part, hidden), jnp.float32)
    total_out = jnp.zeros((hidden, part), jnp.float32)

    def tail(x, g, total_in, total_out):
        x, g = both_halves(x.reshape(rows, half)), both_halves(g.reshape(rows, half))
        pre = jnp.dot(x, full_in, preferred_element_type=jnp.float32)
        sigma = jax.nn.sigmoid(pre)
        act = (pre * sigma).astype(jnp.bfloat16)
        grad_act = times_transposed(g, full_out)
        dpre = (grad_act * sigma * (1.0 + pre * (1.0 - sigma))).astype(jnp.bfloat16)
        x_part = lax.dynamic_slice_in_dim(x, dp_index * part, part, 1)
        g_part = lax.dynamic_slice_in_dim(g, dp_index * part, part, 1)
        return total_in + cross(x_part, dpre), total_out + cross(act, g_part)

    if steps <= 4:
        for i in range(steps):
            total_in, total_out = tail(
                all_saved[i * chunk : (i + 1) * chunk],
                all_grad[i * chunk : (i + 1) * chunk],
                total_in,
                total_out,
            )
    else:
        def body(i, totals):
            x = lax.dynamic_slice_in_dim(all_saved, i * chunk, chunk, 0)
            g = lax.dynamic_slice_in_dim(all_grad, i * chunk, chunk, 0)
            return tail(x, g, *totals)

        total_in, total_out = lax.fori_loop(0, steps, body, (total_in, total_out))
    return (
        grads[None],
        total_in.astype(jnp.bfloat16)[None],
        total_out.astype(jnp.bfloat16)[None],
    )


def solution(mesh):
    return jax.shard_map(
        local,
        mesh=mesh,
        in_specs=(
            P("section", None, "dp", None),
            P(None, "dp", None),
            P("section", "dp", "mp"),
            P("section", "mp", "dp"),
            P(None, "dp"),
        ),
        out_specs=(
            P("section", None, "dp", "mp"),
            P("section", "dp", "mp"),
            P("section", "mp", "dp"),
        ),
        check_vma=False,
    )
```

time: 1170 us -> 668 us (0.57)
  waiting for transfers between devices: 995 us -> 405 us
  matrix products: 64.7 us -> 170 us
  blocking collectives: 14.2 us -> 0 us
    reduce_scatter x8 -> x0, waiting for transfers between devices: 623 us -> none  [the longest x1 279 us: local(): lax.psum_scatter(cross(act_flat, grad_flat), 'dp', scatter_dimension=1, t...]
    dot_general x6, matrix products: 24 us -> 79 us  [times_transposed(): lax.dot_general(left, right, (((1,), (1,)), ((), ())), preferred_element_...]
    all_gather x2 -> x4, waiting for transfers between devices: 301 us -> 331 us  [the longest x1 147 us: local(): full_in = lax.all_gather(weight_in[0], 'dp', axis=0, tiled=True)]
    dot_general x2 -> x6, matrix products: 24 us -> 52.7 us  [cross(): lax.dot_general(left, right, (((0,), (0,)), ((), ())), preferred_element_...]
    dot_general x3 -> x4, matrix products: 16.7 us -> 38.5 us  [the longest x3 27.6 us: tail(): pre = jnp.dot(x, full_in, preferred_element_type=jnp.float32)]
    ppermute x0 -> x18, waiting for transfers between devices: none -> 15.5 us  [swapped(): return lax.ppermute(x, 'mp', [(0, 1), (1, 0)])]
    all_gather x6 -> x0, blocking collectives: 14.2 us -> none  [chain_step(): grad_full = lax.all_gather(own_slice, 'mp', axis=1, tiled=True)]
    ppermute x6 -> x5, waiting for transfers between devices: 69.5 us -> 57.3 us  [passed_along(): return lax.ppermute(x, axis, pairs)]
  transfers between devices with their start and end apart: 16 -> 27, of which waited for: 16 -> 18; matrix products, arithmetic and copies ran while one was open for 3% -> 21% of each run, Pallas kernels for 0% -> 0%
where the time goes in v1:
time: 668 us; the launch traced here: 662 us
  waiting for transfers between devices  405 us (61%)
  matrix products  170 us (25%)
  other arithmetic  37.5 us (6%)
  local copies, waits for them, and re-layouts  23 us (3%)
  between operations  14.8 us (2%)
  starting transfers between devices  11.1 us (2%)
    all_gather x1, waiting for transfers between devices, local(): full_in = lax.all_gather(weight_in[0], 'dp', axis=0, tiled=True)  147 us
    all_gather x1, waiting for transfers between devices, local(): full_out = lax.all_gather(weight_out[0], 'dp', axis=1, tiled=True)  139 us
    dot_general x6, matrix products, times_transposed(): lax.dot_general(left, right, (((1,), (1,)), ((), ())), preferred_element_...  79 us
    ppermute x5, waiting for transfers between devices, passed_along(): return lax.ppermute(x, axis, pairs)  57.3 us
    dot_general x6, matrix products, cross(): lax.dot_general(left, right, (((0,), (0,)), ((), ())), preferred_element_...  52.7 us
    all_gather x1, waiting for transfers between devices, local(): all_grad = lax.all_gather(arrived, 'dp', axis=0, tiled=True)  45.7 us
    dot_general x3, matrix products, tail(): pre = jnp.dot(x, full_in, preferred_element_type=jnp.float32)  27.6 us
    ppermute x18, waiting for transfers between devices, swapped(): return lax.ppermute(x, 'mp', [(0, 1), (1, 0)])  15.5 us
  transfers between devices with their start and end apart: 27, of which 18 were waited for; matrix products, arithmetic and copies ran while one was open for 21% of the time, Pallas kernels for 0%

profile of v1, /device:TPU:0, one launch (start us, length us, event | category | flops | bytes accessed | tf_op | source)
XLA Modules:
  0.0 661.8 jit_solution(3181467652370129304)
XLA Ops:
  8.8 1.5 dynamic-slice_select_fusion
  15.3 146.7 %all-gather.12.cloned.1.call-done = bf16[1,2048,2048]{2,1,0:T(8,128)(2,1)} async-done(((bf16[1,512,2048]{2,1,0:T(8,128)(2,1)}), bf16[1,2048,2048]{2,1,0:T(8,128)(2,1)}) %all-gather.12.cloned.1.call-update) | async-done | bytes 8388624 | tf_op jit(solution)/shard_map/all_gather | solution.py:52
  162.0 10.9 %add_multiply_fusion = f32[576,2048]{1,0:T(8,128)} fusion(bf16[576,2048]{1,0:T(8,128)(2,1)S(1)} %bitcast.209, bf16[1,2048,2048]{2,1,0:T(8,128)(2,1)} %all-gather.12.cloned.1.call-done), kind=kOutput, calls=%fused_computation.47 | convolution fusion | flops 4840095744 | bytes 15466496 | tf_op jit(solution)/shard_map/dot_general | solution.py:58
  172.9 138.6 %all-gather.10.cloned.1.call-done = bf16[1,2048,2048]{2,1,0:T(8,128)(2,1)} async-done(((bf16[1,2048,512]{2,1,0:T(8,128)(2,1)}), bf16[1,2048,2048]{2,1,0:T(8,128)(2,1)}) %all-gather.10.cloned.1.call-update) | async-done | bytes 8388624 | tf_op jit(solution)/shard_map/all_gather | solution.py:53
  311.4 13.1 %fusion.16 = f32[192,2048]{1,0:T(8,128)} fusion(bf16[1,2048,2048]{2,1,0:T(8,128)(2,1)} %all-gather.12.cloned.1.call-done, bf16[1,2048,2048]{2,1,0:T(8,128)(2,1)} %all-gather.10.cloned.1.call-done, f32[3,192,2048]{2,1,0:T(8,128)} %bitcast.220, s32[]{:T(128)S(6)} %min.19, bf16[192,1024]{1,0:T(8,128)(2,1)S(1)} %copy-done.23, ...), kind=kOutput, calls=%fused_computation.16 | convolution fusion | flops 3223584768 | bytes 20709380 | tf_op jit(solution)/shard_map/dot_general | solution.py:24
  325.9 1.7 collective-permute-done.1
  327.7 2.0 bitcast_dynamic-update-slice_fusion
  331.2 11.8 %collective-permute-done.2 = bf16[192,1024]{1,0:T(8,128)(2,1)} collective-permute-done((bf16[192,1024]{1,0:T(8,128)(2,1)}, bf16[192,1024]{1,0:T(8,128)(2,1)}, u32[]{:S(2)}, u32[]{:S(2)}) %collective-permute-start.2) | collective-permute-done | bytes 393248 | tf_op jit(solution)/shard_map/ppermute | solution.py:10
  343.1 2.2 fusion.157
  345.3 1.7 collective-permute-done.3
  348.0 13.3 %fusion.14 = f32[192,2048]{1,0:T(8,128)} fusion(bf16[1,2048,2048]{2,1,0:T(8,128)(2,1)} %all-gather.12.cloned.1.call-done, bf16[1,2048,2048]{2,1,0:T(8,128)(2,1)} %all-gather.10.cloned.1.call-done, f32[3,192,2048]{2,1,0:T(8,128)} %bitcast.221, s32[]{:T(128)S(6)} %min.20, bf16[192,1024]{1,0:T(8,128)(2,1)} %get-tuple-element.52, ...), kind=kOutput, calls=%fused_computation.14 | convolution fusion | flops 3223584768 | bytes 20709380 | tf_op jit(solution)/shard_map/dot_general | solution.py:24
  362.7 1.6 collective-permute-done.4
  364.2 2.3 fusion.161
  367.8 12.7 %collective-permute-done.5 = bf16[192,1024]{1,0:T(8,128)(2,1)} collective-permute-done((bf16[192,1024]{1,0:T(8,128)(2,1)}, bf16[192,1024]{1,0:T(8,128)(2,1)}, u32[]{:S(2)}, u32[]{:S(2)}) %collective-permute-start.5) | collective-permute-done | bytes 393248 | tf_op jit(solution)/shard_map/ppermute | solution.py:10
  380.5 2.4 fusion.156
  386.1 14.1 %fusion.12 = f32[192,2048]{1,0:T(8,128)} fusion(bf16[1,2048,2048]{2,1,0:T(8,128)(2,1)} %all-gather.12.cloned.1.call-done, bf16[1,2048,2048]{2,1,0:T(8,128)(2,1)} %all-gather.10.cloned.1.call-done, f32[3,192,2048]{2,1,0:T(8,128)} %bitcast.222, s32[]{:T(128)S(6)} %min.21, bf16[192,1024]{1,0:T(8,128)(2,1)S(1)} %get-tuple-element.50, ...), kind=kOutput, calls=%fused_computation.12 | convolution fusion | flops 3223584768 | bytes 20709380 | tf_op jit(solution)/shard_map/dot_general | solution.py:24
  401.6 1.7 collective-permute-done.7
  403.2 1.5 fusion.160
  404.8 1.7 collective-permute-start.8
  406.5 12.5 %collective-permute-done.8 = bf16[192,1024]{1,0:T(8,128)(2,1)S(1)} collective-permute-done((bf16[192,1024]{1,0:T(8,128)(2,1)S(1)}, bf16[192,1024]{1,0:T(8,128)(2,1)S(1)}, u32[]{:S(2)}, u32[]{:S(2)}) %collective-permute-start.8) | collective-permute-done | bytes 393248 | tf_op jit(solution)/shard_map/ppermute | solution.py:10
  418.9 2.0 fusion.155
  420.9 1.7 collective-permute-done.9
  423.5 13.2 %fusion.10 = f32[192,2048]{1,0:T(8,128)} fusion(bf16[1,2048,2048]{2,1,0:T(8,128)(2,1)} %all-gather.12.cloned.1.call-done, bf16[1,2048,2048]{2,1,0:T(8,128)(2,1)} %all-gather.10.cloned.1.call-done, f32[3,192,2048]{2,1,0:T(8,128)} %bitcast.223, s32[]{:T(128)S(6)} %min.22, bf16[192,1024]{1,0:T(8,128)(2,1)} %get-tuple-element.48, ...), kind=kOutput, calls=%fused_computation.10 | convolution fusion | flops 3223584768 | bytes 20709380 | tf_op jit(solution)/shard_map/dot_general | solution.py:24
  438.0 1.6 collective-permute-done.10
  442.4 12.7 %collective-permute-done.11 = bf16[192,1024]{1,0:T(8,128)(2,1)S(1)} collective-permute-done((bf16[192,1024]{1,0:T(8,128)(2,1)S(1)}, bf16[192,1024]{1,0:T(8,128)(2,1)S(1)}, u32[]{:S(2)}, u32[]{:S(2)}) %collective-permute-start.11) | collective-permute-done | bytes 393248 | tf_op jit(solution)/shard_map/ppermute | solution.py:10
  455.0 2.0 fusion.154
  457.0 1.7 collective-permute-done.12
  459.5 13.1 %fusion.8 = f32[192,2048]{1,0:T(8,128)} fusion(bf16[1,2048,2048]{2,1,0:T(8,128)(2,1)} %all-gather.12.cloned.1.call-done, bf16[1,2048,2048]{2,1,0:T(8,128)(2,1)} %all-gather.10.cloned.1.call-done, f32[3,192,2048]{2,1,0:T(8,128)} %bitcast.224, s32[]{:T(128)S(6)} %min.23, bf16[192,1024]{1,0:T(8,128)(2,1)} %get-tuple-element.46, ...), kind=kOutput, calls=%fused_computation.8 | convolution fusion | flops 3223584768 | bytes 20709380 | tf_op jit(solution)/shard_map/dot_general | solution.py:24
  474.0 1.6 collective-permute-done.13
  478.6 4.7 fusion.206
  483.3 7.6 %collective-permute-done.14 = bf16[192,1024]{1,0:T(8,128)(2,1)S(1)} collective-permute-done((bf16[192,1024]{1,0:T(8,128)(2,1)S(1)}, bf16[192,1024]{1,0:T(8,128)(2,1)S(1)}, u32[]{:S(2)}, u32[]{:S(2)}) %collective-permute-start.14) | collective-permute-done | bytes 393248 | tf_op jit(solution)/shard_map/ppermute | solution.py:10
  491.0 2.0 fusion.153
  493.6 3.9 broadcast_select_fusion.11
  497.5 1.9 broadcast_select_fusion.7
  499.7 3.5 broadcast_select_fusion.2
  503.2 8.7 %fusion = f32[768,2048]{1,0:T(8,128)} fusion(bf16[1,2048,2048]{2,1,0:T(8,128)(2,1)S(1)} %bitcast.218, bf16[768,1024]{1,0:T(8,128)(2,1)S(1)} %get-tuple-element.31, bf16[768,1024]{1,0:T(8,128)(2,1)S(1)} %get-tuple-element.32), kind=kOutput, calls=%fused_computation | convolution fusion | flops 6448742400 | bytes 17825792 | tf_op jit(solution)/shard_map/dot_general | solution.py:98
  511.9 8.7 %fusion.2 = f32[768,2048]{1,0:T(8,128)} fusion(bf16[1,2048,2048]{2,1,0:T(8,128)(2,1)S(1)} %bitcast.218, bf16[768,1024]{1,0:T(8,128)(2,1)S(1)} %get-tuple-element.36, bf16[768,1024]{1,0:T(8,128)(2,1)S(1)} %get-tuple-element.35), kind=kOutput, calls=%fused_computation.2 | convolution fusion | flops 6448742400 | bytes 17825792 | tf_op jit(solution)/shard_map/dot_general | solution.py:98
  521.6 12.3 %fusion.6 = f32[192,2048]{1,0:T(8,128)S(1)} fusion(bf16[1,2048,2048]{2,1,0:T(8,128)(2,1)} %all-gather.12.cloned.1.call-done, bf16[1,2048,2048]{2,1,0:T(8,128)(2,1)} %all-gather.10.cloned.1.call-done, f32[3,192,2048]{2,1,0:T(8,128)} %bitcast.225, s32[]{:T(128)S(6)} %min.24, bf16[192,1024]{1,0:T(8,128)(2,1)} %get-tuple-element.44, ...), kind=kOutput, calls=%fused_computation.6 | convolution fusion | flops 3223584768 | bytes 20709380 | tf_op jit(solution)/shard_map/dot_general | solution.py:24
  535.3 45.7 %all-gather.8.cloned.1.call-done = bf16[12,192,1024]{2,1,0:T(8,128)(2,1)} async-done(((bf16[3,192,1024]{2,1,0:T(8,128)(2,1)}), bf16[12,192,1024]{2,1,0:T(8,128)(2,1)}) %all-gather.8.cloned.1.call-update) | async-done | bytes 4718608 | tf_op jit(solution)/shard_map/all_gather | solution.py:87
  581.0 2.9 fusion.205
  583.9 10.2 %fusion.4 = f32[768,2048]{1,0:T(8,128)S(1)} fusion(bf16[1,2048,2048]{2,1,0:T(8,128)(2,1)} %all-gather.12.cloned.1.call-done, bf16[768,1024]{1,0:T(8,128)(2,1)} %get-tuple-element.40, bf16[768,1024]{1,0:T(8,128)(2,1)} %get-tuple-element.39), kind=kOutput, calls=%fused_computation.4 | convolution fusion | flops 6448742400 | bytes 17825792 | tf_op jit(solution)/shard_map/dot_general | solution.py:98
  594.8 1.9 copy-done.21
  598.4 2.1 fusion.44
  602.2 2.1 fusion.45
  606.4 3.6 fusion.48
  610.0 14.6 %fusion.88 = f32[512,2048]{1,0:T(8,128)} fusion(f32[768,2048]{1,0:T(8,128)} %copy-done.25, bf16[1,2048,2048]{2,1,0:T(8,128)(2,1)} %all-gather.10.cloned.1.call-done, bf16[768,1024]{1,0:T(8,128)(2,1)} %copy-done.14, bf16[768,1024]{1,0:T(8,128)(2,1)} %copy-done.13, s32[]{:T(128)S(6)} %select_n.355, bf16[768,1024]{1,0:T(8,128)(2,1)S(1)} %copy-done.8, ...), kind=kOutput, calls=%fused_computation.97 | convolution fusion | flops 8075083776 | bytes 25165828 | tf_op jit(solution)/shard_map/dot_general | solution.py:18
  624.6 14.6 %fusion.91 = f32[512,2048]{1,0:T(8,128)} fusion(f32[768,2048]{1,0:T(8,128)} %fusion.2, bf16[1,2048,2048]{2,1,0:T(8,128)(2,1)} %all-gather.10.cloned.1.call-done, bf16[768,1024]{1,0:T(8,128)(2,1)} %copy-done.16, bf16[768,1024]{1,0:T(8,128)(2,1)} %copy-done.15, s32[]{:T(128)S(6)} %select_n.355, bf16[768,1024]{1,0:T(8,128)(2,1)} %copy-done.9, ...), kind=kOutput, calls=%fused_computation.98 | convolution fusion | flops 8075083776 | bytes 25165828 | tf_op jit(solution)/shard_map/dot_general | solution.py:18
  639.2 15.6 %fusion.47 = bf16[1,512,2048]{2,1,0:T(8,128)(2,1)} fusion(f32[512,2048]{1,0:T(8,128)} %fusion.88, f32[512,2048]{1,0:T(8,128)} %fusion.91, s32[]{:T(128)S(6)} %select_n.355, bf16[768,1024]{1,0:T(8,128)(2,1)} %copy-done.12, bf16[768,1024]{1,0:T(8,128)(2,1)} %copy-done.11, f32[768,2048]{1,0:T(8,128)} %fusion, ...), kind=kOutput, calls=%fused_computation.71 | convolution fusion | flops 8078229504 | bytes 31457284 | tf_op jit(solution)/shard_map/dot_general | solution.py:18
  (131 shorter events, 37.0 us)
Async XLA Ops:
  7.2 154.8 %copy-start = (bf16[1,3,192,2048]{3,2,1,0:T(8,128)(2,1)S(1)}, bf16[1,3,192,2048]{3,2,1,0:T(8,128)(2,1)}, u32[]{:S(2)}) copy-start(bf16[1,3,192,2048]{3,2,1,0:T(8,128)(2,1)} %param.5) | copy-start | bytes 7077892
  7.2 154.8 %all-gather.12.cloned.1.call-start = ((), (), s32[]{:S(2)}) async-start(), calls=%async_computation.2 | async-start | bytes 10485760 | tf_op jit(solution)/shard_map/all_gather | solution.py:52
  7.9 303.5 %all-gather.10.cloned.1.call-start = ((), (), s32[]{:S(2)}) async-start(), calls=%async_computation.1 | async-start | bytes 10485760 | tf_op jit(solution)/shard_map/all_gather | solution.py:53
  8.7 469.9 %all-gather.14.cloned.1.call-start = ((), (), s32[]{:S(2)}) async-start(), calls=%async_computation.3 | async-start | bytes 5898240 | tf_op jit(solution)/shard_map/all_gather | solution.py:85
  12.7 160.2 %copy-start.6 = (bf16[192,1024]{1,0:T(8,128)(2,1)}, bf16[192,1024]{1,0:T(8,128)(2,1)S(1)}, u32[]{:S(2)}) copy-start(bf16[192,1024]{1,0:T(8,128)(2,1)S(1)} %get-tuple-element.42) | copy-start | bytes 1179652
  12.7 1.8 collective-permute-start
  162.0 149.5 %copy-start.23 = (bf16[192,1024]{1,0:T(8,128)(2,1)S(1)}, bf16[192,1024]{1,0:T(8,128)(2,1)}, u32[]{:S(2)}) copy-start(bf16[192,1024]{1,0:T(8,128)(2,1)} %get-tuple-element.54) | copy-start | bytes 1179652
  324.5 3.2 copy-start.22
  325.8 1.8 collective-permute-start.1
  329.7 13.4 %collective-permute-start.2 = (bf16[192,1024]{1,0:T(8,128)(2,1)}, bf16[192,1024]{1,0:T(8,128)(2,1)}, u32[]{:S(2)}, u32[]{:S(2)}) collective-permute-start(bf16[192,1024]{1,0:T(8,128)(2,1)} %get-tuple-element.22), channel_id=1, source_target_pairs={{8,0},{16,8},{24,16},{9,1},{17,9},{25,17},{10,2},{18,10},{26,18},{... | collective-permute-start | bytes 1179656 | tf_op jit(solution)/shard_map/ppermute | solution.py:10
  345.3 1.7 collective-permute-start.3
  362.5 1.8 collective-permute-start.4
  366.5 14.0 %collective-permute-start.5 = (bf16[192,1024]{1,0:T(8,128)(2,1)}, bf16[192,1024]{1,0:T(8,128)(2,1)}, u32[]{:S(2)}, u32[]{:S(2)}) collective-permute-start(bf16[192,1024]{1,0:T(8,128)(2,1)} %get-tuple-element.20), channel_id=1, source_target_pairs={{8,0},{16,8},{24,16},{9,1},{17,9},{25,17},{10,2},{18,10},{26,18},{... | collective-permute-start | bytes 1179656 | tf_op jit(solution)/shard_map/ppermute | solution.py:10
  382.9 2.1 collective-permute-start.6
  384.0 196.9 %all-gather.8.cloned.1.call-start = ((), (), s32[]{:S(2)}) async-start(), calls=%async_computation | async-start | bytes 5898240 | tf_op jit(solution)/shard_map/all_gather | solution.py:87
  400.2 18.8 %copy-start.3 = (bf16[3,192,1024]{2,1,0:T(8,128)(2,1)S(1)}, bf16[3,192,1024]{2,1,0:T(8,128)(2,1)}, u32[]{:S(2)}) copy-start(bf16[3,192,1024]{2,1,0:T(8,128)(2,1)} %copy-done.2) | copy-start | bytes 3538948
  401.4 1.8 collective-permute-start.7
  404.8 14.2 %collective-permute-start.8 = (bf16[192,1024]{1,0:T(8,128)(2,1)S(1)}, bf16[192,1024]{1,0:T(8,128)(2,1)S(1)}, u32[]{:S(2)}, u32[]{:S(2)}) collective-permute-start(bf16[192,1024]{1,0:T(8,128)(2,1)S(1)} %get-tuple-element.18), channel_id=1, source_target_pairs={{8,0},{16,8},{24,16},{9,1},{17,9},{25,17},{10,2},{18,10},{26,18},{... | collective-permute-start | bytes 1179656 | tf_op jit(solution)/shard_map/ppermute | solution.py:10
  420.9 1.7 collective-permute-start.9
  437.8 1.8 collective-permute-start.10
  441.0 14.0 %collective-permute-start.11 = (bf16[192,1024]{1,0:T(8,128)(2,1)S(1)}, bf16[192,1024]{1,0:T(8,128)(2,1)S(1)}, u32[]{:S(2)}, u32[]{:S(2)}) collective-permute-start(bf16[192,1024]{1,0:T(8,128)(2,1)S(1)} %get-tuple-element.16), channel_id=1, source_target_pairs={{8,0},{16,8},{24,16},{9,1},{17,9},{25,17},{10,2},{18,10},{26,18},{... | collective-permute-start | bytes 1179656 | tf_op jit(solution)/shard_map/ppermute | solution.py:10
  457.0 1.7 collective-permute-start.12
  473.8 1.8 collective-permute-start.13
  477.0 13.9 %collective-permute-start.14 = (bf16[192,1024]{1,0:T(8,128)(2,1)S(1)}, bf16[192,1024]{1,0:T(8,128)(2,1)S(1)}, u32[]{:S(2)}, u32[]{:S(2)}) collective-permute-start(bf16[192,1024]{1,0:T(8,128)(2,1)S(1)} %get-tuple-element.14), channel_id=1, source_target_pairs={{8,0},{16,8},{24,16},{9,1},{17,9},{25,17},{10,2},{18,10},{26,18},{... | collective-permute-start | bytes 1179656 | tf_op jit(solution)/shard_map/ppermute | solution.py:10
  483.2 10.4 %collective-permute-start.17 = (bf16[768,1024]{1,0:T(8,128)(2,1)}, bf16[768,1024]{1,0:T(8,128)(2,1)}, u32[]{:S(2)}, u32[]{:S(2)}) collective-permute-start(bf16[768,1024]{1,0:T(8,128)(2,1)} %bitcast.26), channel_id=1, source_target_pairs={{0,1},{1,0},{2,3},{3,2},{4,5},{5,4},{6,7},{7,6},{8,9},{9,8},{10,11... | collective-permute-start | bytes 4718600 | tf_op jit(solution)/shard_map/ppermute | solution.py:14
  493.0 4.5 collective-permute-start.19
  493.1 6.3 collective-permute-start.21
  493.6 3.9 copy-start.5
  493.6 9.6 %slice-start = ((s8[8388608]{0:T(1024)(128)(4,1)}), s8[4194304]{0:T(1024)(128)(4,1)S(1)}, s32[]{:S(2)}) async-start(s8[8388608]{0:T(1024)(128)(4,1)} %bitcast.217), calls=%async_computation.4 | async-start | bytes 8388608
  497.5 5.7 slice-start.1
  499.4 12.5 %copy-start.9 = (bf16[768,1024]{1,0:T(8,128)(2,1)}, bf16[768,1024]{1,0:T(8,128)(2,1)S(1)}, u32[]{:S(2)}) copy-start(bf16[768,1024]{1,0:T(8,128)(2,1)S(1)} %get-tuple-element.35) | copy-start | bytes 4718596
  499.4 12.5 %copy-start.10 = (bf16[768,1024]{1,0:T(8,128)(2,1)}, bf16[768,1024]{1,0:T(8,128)(2,1)S(1)}, u32[]{:S(2)}) copy-start(bf16[768,1024]{1,0:T(8,128)(2,1)S(1)} %get-tuple-element.36) | copy-start | bytes 4718596
  503.2 8.7 %copy-start.11 = (bf16[768,1024]{1,0:T(8,128)(2,1)}, bf16[768,1024]{1,0:T(8,128)(2,1)S(1)}, u32[]{:S(2)}) copy-start(bf16[768,1024]{1,0:T(8,128)(2,1)S(1)} %get-tuple-element.31) | copy-start | bytes 4718596
  503.2 8.7 %copy-start.12 = (bf16[768,1024]{1,0:T(8,128)(2,1)}, bf16[768,1024]{1,0:T(8,128)(2,1)S(1)}, u32[]{:S(2)}) copy-start(bf16[768,1024]{1,0:T(8,128)(2,1)S(1)} %get-tuple-element.32) | copy-start | bytes 4718596
  511.9 8.8 %collective-permute-start.15 = (bf16[192,1024]{1,0:T(8,128)(2,1)S(1)}, bf16[192,1024]{1,0:T(8,128)(2,1)S(1)}, u32[]{:S(2)}, u32[]{:S(2)}) collective-permute-start(bf16[192,1024]{1,0:T(8,128)(2,1)S(1)} %get-tuple-element.4), channel_id=1, source_target_pairs={{0,1},{1,0},{2,3},{3,2},{4,5},{5,4},{6,7},{7,6},{8,9},{9,8},{10,11... | collective-permute-start | bytes 1179656 | tf_op jit(solution)/shard_map/ppermute | solution.py:14
  534.8 60.0 %collective-permute-start.16 = (bf16[192,1024]{1,0:T(8,128)(2,1)}, bf16[192,1024]{1,0:T(8,128)(2,1)S(1)}, u32[]{:S(2)}, u32[]{:S(2)}) collective-permute-start(bf16[192,1024]{1,0:T(8,128)(2,1)} %dynamic-slice_convert_fusion), channel_id=1, source_target_pairs={{0,1},{1,0},{2,3},{3,2},{4,5},{5,4},{6,7},{7,6},{8,9},{9,8},{10,11... | collective-permute-start | bytes 1179656 | tf_op jit(solution)/shard_map/ppermute | solution.py:14
  583.8 14.2 %collective-permute-start.18 = (bf16[768,1024]{1,0:T(8,128)(2,1)S(1)}, bf16[768,1024]{1,0:T(8,128)(2,1)S(1)}, u32[]{:S(2)}, u32[]{:S(2)}) collective-permute-start(bf16[768,1024]{1,0:T(8,128)(2,1)S(1)} %bitcast.216), channel_id=1, source_target_pairs={{0,1},{1,0},{2,3},{3,2},{4,5},{5,4},{6,7},{7,6},{8,9},{9,8},{10,11... | collective-permute-start | bytes 4718600 | tf_op jit(solution)/shard_map/ppermute | solution.py:14
  594.2 6.4 copy-start.25
  594.3 6.3 collective-permute-start.20
  597.0 7.4 %collective-permute-start.22 = (bf16[768,1024]{1,0:T(8,128)(2,1)S(1)}, bf16[768,1024]{1,0:T(8,128)(2,1)S(1)}, u32[]{:S(2)}, u32[]{:S(2)}) collective-permute-start(bf16[768,1024]{1,0:T(8,128)(2,1)S(1)} %bitcast.214), channel_id=1, source_target_pairs={{0,1},{1,0},{2,3},{3,2},{4,5},{5,4},{6,7},{7,6},{8,9},{9,8},{10,11... | collective-permute-start | bytes 4718600 | tf_op jit(solution)/shard_map/ppermute | solution.py:14
  598.0 2.9 slice-start.2
  598.3 3.9 slice-start.3
  600.5 5.8 slice-start.4
  600.9 3.5 copy-start.15
  600.9 3.5 copy-start.16
  602.2 4.2 slice-start.5
  606.4 3.6 copy-start.8
  639.2 15.6 %copy-start.1 = (bf16[1,3,192,2048]{3,2,1,0:T(8,128)(2,1)S(1)}, bf16[1,3,192,2048]{3,2,1,0:T(8,128)(2,1)}, u32[]{:S(2)}) copy-start(bf16[1,3,192,2048]{3,2,1,0:T(8,128)(2,1)} %param.5) | copy-start | bytes 7077892
  (11 other events, 19.1 us)
Sparse Core Ops, SparseCore 0:
  9.6 152.3 all-gather.11
  163.5 147.8 all-gather.9
  384.2 87.9 all-gather.13
  493.1 87.8 all-gather.7

commit v2 on v1

--- a/solution.py
+++ b/solution.py
@@ -1,6 +1,10 @@
+import functools
+
 import jax
 import jax.numpy as jnp
 from jax import lax
+from jax.experimental import pallas as pl
+from jax.experimental.pallas import tpu as pltpu
 from jax.sharding import PartitionSpec as P
 
 
@@ -35,6 +39,235 @@
 def slope(pre):
     sigma = jax.nn.sigmoid(pre)
     return sigma * (1.0 + pre * (1.0 - sigma))
+
+
+MESH = pl.DeviceIdType.MESH
+TILE = 512
+
+
+def chain_kernel(
+    sections, replicas, w_in, w_out, slopes, first, own_x,
+    grads, all_x, all_g,
+    g_buf, dpre, mine, give, take,
+    hop_send, hop_recv, fwd_send, fwd_recv, swap_send, swap_recv,
+    x_send, x_recv, g_send, g_recv, own_sem,
+):
+    section = lax.axis_index("section")
+    place = lax.axis_index("dp")
+    core = lax.axis_index("mp")
+    micros, _, rows, half = g_buf.shape
+    hidden = dpre.shape[1]
+    last = sections - 1
+
+    barrier = pltpu.get_barrier_semaphore()
+    greeted = [{"mp": 1 - core}]
+    greeted += [{"dp": lax.rem(place + step, replicas)} for step in (1, replicas - 1)]
+    greeted += [{"section": lax.rem(section + step, sections)} for step in (1, sections - 1)]
+    for device in greeted:
+        pl.semaphore_signal(barrier, inc=1, device_id=device, device_id_type=MESH)
+    pl.semaphore_wait(barrier, len(greeted))
+
+    def remote(src, dst, send, recv, device):
+        return pltpu.make_async_remote_copy(
+            src_ref=src, dst_ref=dst, send_sem=send, recv_sem=recv,
+            device_id=device, device_id_type=MESH,
+        )
+
+    def sent(way, k):
+        origin = place - (k - 1) if way == 0 else place + (k - 1)
+        to = place + 1 if way == 0 else place - 1
+        ok = (origin >= 0) & (origin < replicas) & (to >= 0) & (to < replicas)
+        return jnp.clip(origin, 0, replicas - 1), jnp.clip(to, 0, replicas - 1), ok
+
+    def came(way, k):
+        origin = place - k if way == 0 else place + k
+        return jnp.clip(origin, 0, replicas - 1), (origin >= 0) & (origin < replicas)
+
+    def x_copy(way, k, origin, to):
+        src = own_x if k == 1 else all_x.at[origin]
+        return remote(
+            src, all_x.at[origin], x_send.at[way, k - 1], x_recv.at[way, k - 1], {"dp": to}
+        )
+
+    def g_copy(way, k, m, origin, to):
+        src = g_buf.at[m, core] if k == 1 else all_g.at[origin, m]
+        return remote(
+            src, all_g.at[origin, m], g_send.at[way, k - 1, m], g_recv.at[way, k - 1, m],
+            {"dp": to},
+        )
+
+    def start(copy_of, k, *m):
+        for way in range(2):
+            origin, to, ok = sent(way, k)
+
+            @pl.when(ok)
+            def _():
+                copy_of(way, k, *m, origin, to).start()
+
+    def landed(copy_of, k, *m):
+        for way in range(2):
+            origin, ok = came(way, k)
+
+            @pl.when(ok)
+            def _():
+                copy_of(way, k, *m, origin, origin).wait_recv()
+
+    def left(copy_of, k, *m):
+        for way in range(2):
+            origin, to, ok = sent(way, k)
+
+            @pl.when(ok)
+            def _():
+                copy_of(way, k, *m, origin, to).wait_send()
+
+    def hop(m):
+        return remote(
+            grads.at[m], g_buf.at[m, core], hop_send.at[m], hop_recv.at[m],
+            {"section": jnp.maximum(section - 1, 0)},
+        )
+
+    def forward(m, which):
+        return remote(
+            g_buf.at[m, which], g_buf.at[m, which], fwd_send.at[m], fwd_recv.at[m],
+            {"mp": 1 - core},
+        )
+
+    def swap(m):
+        return remote(
+            give.at[m], take.at[m], swap_send.at[m], swap_recv.at[m], {"mp": 1 - core}
+        )
+
+    def own_copies(m):
+        return pltpu.make_async_copy(g_buf.at[m, core], all_g.at[place, m], own_sem.at[m])
+
+    def nt(left_block, right_block):
+        return lax.dot_general(
+            left_block, right_block, (((1,), (1,)), ((), ())),
+            preferred_element_type=jnp.float32,
+        )
+
+    start(x_copy, 1)
+    x_own = pltpu.make_async_copy(own_x, all_x.at[place], own_sem.at[micros])
+    x_own.start()
+    for k in range(2, replicas):
+
+        @pl.when(section <= last - k)
+        def _():
+            landed(x_copy, k - 1)
+            start(x_copy, k)
+
+    for m in range(micros):
+
+        @pl.when(section == last)
+        def _():
+            g_buf[m] = first[m]
+
+        @pl.when(section < last)
+        def _():
+            hop(m).wait_recv()
+            forward(m, core).start()
+
+        start(g_copy, 1, m)
+        own_copies(m).start()
+
+        @pl.when(section < last)
+        def _():
+            forward(m, 1 - core).wait_recv()
+
+        @pl.loop(0, hidden // TILE)
+        def _(j):
+            at = pl.ds(pl.multiple_of(j * TILE, TILE), TILE)
+            total = nt(g_buf[m, 0], w_out[at, :half]) + nt(g_buf[m, 1], w_out[at, half:])
+            dpre[:, at] = (total * slopes[m, :, at]).astype(jnp.bfloat16)
+
+        @pl.loop(0, half // TILE)
+        def _(j):
+            at = pl.ds(pl.multiple_of(j * TILE, TILE), TILE)
+            there = pl.ds(pl.multiple_of((1 - core) * half + j * TILE, TILE), TILE)
+            give[m, :, at] = nt(dpre[...], w_in[there, :]).astype(jnp.bfloat16)
+
+        swap(m).start()
+
+        @pl.loop(0, half // TILE)
+        def _(j):
+            at = pl.ds(pl.multiple_of(j * TILE, TILE), TILE)
+            here = pl.ds(pl.multiple_of(core * half + j * TILE, TILE), TILE)
+            mine[:, at] = nt(dpre[...], w_in[here, :])
+
+        swap(m).wait_recv()
+        grads[m] = (
+            g_buf[m, core].astype(jnp.float32) + (mine[...] + take[m].astype(jnp.float32))
+        ).astype(jnp.bfloat16)
+
+        @pl.when(section > 0)
+        def _():
+            hop(m).start()
+
+    for k in range(2, replicas):
+
+        @pl.when(section > last - k)
+        def _():
+            landed(x_copy, k - 1)
+            start(x_copy, k)
+
+    for k in range(2, replicas):
+        for m in range(micros):
+            landed(g_copy, k - 1, m)
+            start(g_copy, k, m)
+    landed(x_copy, replicas - 1)
+    for m in range(micros):
+        landed(g_copy, replicas - 1, m)
+    x_own.wait()
+    for m in range(micros):
+        own_copies(m).wait()
+        swap(m).wait_send()
+
+        @pl.when(section < last)
+        def _():
+            forward(m, core).wait_send()
+
+        @pl.when(section > 0)
+        def _():
+            hop(m).wait_send()
+
+    for k in range(1, replicas):
+        left(x_copy, k)
+        for m in range(micros):
+            left(g_copy, k, m)
+
+
+def chain(sections, replicas, full_in, full_out, slopes, first, own_x):
+    micros, cores, rows, half = first.shape
+    hidden = full_out.shape[0]
+    vmem, hbm = pl.BlockSpec(memory_space=pltpu.VMEM), pl.BlockSpec(memory_space=pl.ANY)
+    dma = pltpu.SemaphoreType.DMA
+    everyone = jax.ShapeDtypeStruct((replicas, micros, rows, half), jnp.bfloat16)
+    block = (micros, rows, half)
+    return pl.pallas_call(
+        functools.partial(chain_kernel, sections, replicas),
+        out_shape=(jax.ShapeDtypeStruct(block, jnp.bfloat16), everyone, everyone),
+        in_specs=[vmem, vmem, vmem, vmem, hbm],
+        out_specs=(vmem, hbm, hbm),
+        scratch_shapes=[
+            pltpu.VMEM(first.shape, jnp.bfloat16),
+            pltpu.VMEM((rows, hidden), jnp.bfloat16),
+            pltpu.VMEM((rows, half), jnp.float32),
+            pltpu.VMEM(block, jnp.bfloat16),
+            pltpu.VMEM(block, jnp.bfloat16),
+        ]
+        + [dma((micros,))] * 6
+        + [dma((2, replicas - 1))] * 2
+        + [dma((2, replicas - 1, micros))] * 2
+        + [dma((micros + 1,))],
+        compiler_params=pltpu.CompilerParams(
+            collective_id=0, has_side_effects=True, vmem_limit_bytes=56 * 1024 * 1024
+        ),
+        cost_estimate=pl.CostEstimate(
+            flops=8 * micros * rows * half * hidden * cores,
+            bytes_accessed=8 * full_in.size,
+            transcendentals=0,
+        ),
+    )(full_in, full_out, slopes, first, own_x)
 
 
 def local(activations, out_grad, weight_in, weight_out, lengths):
@@ -52,39 +285,16 @@
     full_in = lax.all_gather(weight_in[0], "dp", axis=0, tiled=True)
     full_out = lax.all_gather(weight_out[0], "dp", axis=1, tiled=True)
     valid = jnp.arange(row_count)[None, :] < lengths
-    own_grad = lax.dynamic_slice_in_dim(out_grad, mp_index * half, half, 2)
-    own_grad = jnp.where(valid[..., None], own_grad, jnp.zeros_like(own_grad))
     own_saved = lax.dynamic_slice_in_dim(saved, mp_index * half, half, 2)
     pre = jnp.dot(saved.reshape(-1, width), full_in, preferred_element_type=jnp.float32)
     slopes = slope(pre).reshape(micro_count, row_count, hidden)
 
-    incoming = jnp.zeros((row_count, half), jnp.bfloat16)
-    grads = jnp.zeros((micro_count, row_count, half), jnp.bfloat16)
-    arrived = jnp.zeros((micro_count, row_count, half), jnp.bfloat16)
-    for clock in range(sections + micro_count - 1):
-        micro = clock - (sections - 1 - section_index)
-        active = (micro >= 0) & (micro < micro_count)
-        slot = jnp.clip(micro, 0, micro_count - 1)
-        first = lax.dynamic_index_in_dim(own_grad, slot, 0, keepdims=False)
-        own = jnp.where(section_index == sections - 1, first, incoming)
-        grad_act = times_transposed(both_halves(own), full_out)
-        scale = lax.dynamic_index_in_dim(slopes, slot, 0, keepdims=False)
-        dpre = (grad_act * scale).astype(jnp.bfloat16)
-        terms = times_transposed(dpre, full_in)
-        mine = lax.dynamic_slice_in_dim(terms, mp_index * half, half, 1)
-        theirs = lax.dynamic_slice_in_dim(terms, (1 - mp_index) * half, half, 1)
-        result = own.astype(jnp.float32) + (
-            mine + swapped(theirs.astype(jnp.bfloat16)).astype(jnp.float32)
-        )
-        result = result.astype(jnp.bfloat16)
-        if clock < sections + micro_count - 2:
-            incoming = passed_along(result, "section", -1)
-        grads = jnp.where(active, lax.dynamic_update_index_in_dim(grads, result, slot, 0), grads)
-        arrived = jnp.where(active, lax.dynamic_update_index_in_dim(arrived, own, slot, 0), arrived)
-
-    all_saved = lax.all_gather(own_saved, "dp", axis=0, tiled=True)
+    first = out_grad.reshape(micro_count, row_count, mp_count, half)
+    first = jnp.where(valid[..., None, None], first, jnp.zeros_like(first)).transpose(0, 2, 1, 3)
+    grads, all_saved, all_grad = chain(
+        sections, dp_count, full_in, full_out, slopes, first, own_saved
+    )
     all_saved = all_saved.reshape(-1, row_count, half)
-    all_grad = lax.all_gather(arrived, "dp", axis=0, tiled=True)
     all_grad = all_grad.reshape(-1, row_count, half)
 
     chunk = min(4, dp_count)

time: 668 us -> 595 us (0.89)
  Pallas kernels: 0 us -> 168 us
  waiting for transfers between devices: 405 us -> 291 us
  matrix products: 170 us -> 95.9 us
  other arithmetic: 37.5 us -> 5.45 us
  local copies, waits for them, and re-layouts: 23 us -> 13.1 us
  starting transfers between devices: 11.1 us -> 1.38 us
    pallas_call x0 -> x1, Pallas kernels: none -> 168 us  [chain(): pl.pallas_call(functools.partial(chain_kernel, sections, replicas), out_s...]
    dot_general x6 -> x0, matrix products: 79 us -> none  [times_transposed(): lax.dot_general(left, right, (((1,), (1,)), ((), ())), preferred_element_...]
    ppermute x5 -> x0, waiting for transfers between devices: 57.3 us -> none  [passed_along(): return lax.ppermute(x, axis, pairs)]
    all_gather x2 -> x0, waiting for transfers between devices: 45.7 us -> none  [the longest x1 45.7 us: local(): all_grad = lax.all_gather(arrived, 'dp', axis=0, tiled=True)]
    select_n x14 -> x0, other arithmetic: 25.3 us -> none  [the longest x6 11.5 us: local(): jnp.where(active, lax.dynamic_update_index_in_dim(arrived, own, slot, 0),...]
    ppermute x18 -> x6, waiting for transfers between devices: 15.5 us -> 1.95 us  [swapped(): return lax.ppermute(x, 'mp', [(0, 1), (1, 0)])]
    select_n x11 -> x6, other arithmetic: 12.2 us -> 3.78 us  [both_halves(): jnp.where(first, x, other)]
    ppermute x5 -> x0, starting transfers between devices: 7.23 us -> none  [passed_along(): return lax.ppermute(x, axis, pairs)]
  transfers between devices with their start and end apart: 27 -> 8, of which waited for: 18 -> 3; matrix products, arithmetic and copies ran while one was open for 21% -> 8% of each run, Pallas kernels for 0% -> 0%
where the time goes in v2:
time: 595 us; the launch traced here: 589 us
  waiting for transfers between devices  291 us (49%)
  Pallas kernels  168 us (28%)
  matrix products  95.9 us (16%)
  between operations  14.9 us (3%)
  local copies, waits for them, and re-layouts  13.1 us (2%)
    pallas_call x1, Pallas kernels, chain(): pl.pallas_call(functools.partial(chain_kernel, sections, replicas), out_s...  168 us
    all_gather x1, waiting for transfers between devices, local(): full_in = lax.all_gather(weight_in[0], 'dp', axis=0, tiled=True)  149 us
    all_gather x1, waiting for transfers between devices, local(): full_out = lax.all_gather(weight_out[0], 'dp', axis=1, tiled=True)  138 us
    dot_general x6, matrix products, cross(): lax.dot_general(left, right, (((0,), (0,)), ((), ())), preferred_element_...  57.4 us
    dot_general x3, matrix products, tail(): pre = jnp.dot(x, full_in, preferred_element_type=jnp.float32)  27.5 us
  transfers between devices with their start and end apart: 8, of which 3 were waited for; matrix products, arithmetic and copies ran while one was open for 8% of the time, Pallas kernels for 0%

profile of v2, /device:TPU:0, one launch (start us, length us, event | category | flops | bytes accessed | tf_op | source)
XLA Modules:
  0.0 589.5 jit_solution(6528353602175379203)
XLA Ops:
  7.2 0.0 copy-start
  7.2 0.0 all-gather.5.cloned.1.call-start
  7.2 0.7 all-gather.5.cloned.1.call-update
  7.9 0.0 all-gather.7.cloned.1.call-start
  8.0 0.7 all-gather.7.cloned.1.call-update
  8.7 0.2 copy-done
  8.8 1.1 dynamic-slice_bitcast_fusion.own_x
  10.0 0.1 iota_compare_fusion
  10.0 0.9 copy-done.2
  10.9 1.6 fusion.8.first
  12.5 149.4 %all-gather.5.cloned.1.call-done = bf16[1,2048,2048]{2,1,0:T(8,128)(2,1)} async-done(((bf16[1,512,2048]{2,1,0:T(8,128)(2,1)}), bf16[1,2048,2048]{2,1,0:T(8,128)(2,1)}) %all-gather.5.cloned.1.call-update) | async-done | bytes 8388624 | tf_op jit(solution)/shard_map/all_gather | solution.py:285
  162.0 11.0 %add_multiply_fusion = f32[576,2048]{1,0:T(8,128)} fusion(bf16[576,2048]{1,0:T(8,128)(2,1)S(1)} %bitcast.59, bf16[1,2048,2048]{2,1,0:T(8,128)(2,1)} %all-gather.5.cloned.1.call-done), kind=kOutput, calls=%fused_computation.9 | convolution fusion | flops 4840095744 | bytes 15466496 | tf_op jit(solution)/shard_map/dot_general | solution.py:289
  173.0 138.5 %all-gather.7.cloned.1.call-done = bf16[1,2048,2048]{2,1,0:T(8,128)(2,1)} async-done(((bf16[1,2048,512]{2,1,0:T(8,128)(2,1)}), bf16[1,2048,2048]{2,1,0:T(8,128)(2,1)}) %all-gather.7.cloned.1.call-update) | async-done | bytes 8388624 | tf_op jit(solution)/shard_map/all_gather | solution.py:286
  311.4 167.6 %shard_map.79 = (bf16[3,192,1024]{2,1,0:T(8,128)(2,1)}, bf16[4,3,192,1024]{3,2,1,0:T(8,128)(2,1)}, bf16[4,3,192,1024]{3,2,1,0:T(8,128)(2,1)}) custom-call(bf16[2048,2048]{1,0:T(8,128)(2,1)} %bitcast.70, bf16[2048,2048]{1,0:T(8,128)(2,1)} %bitcast.69, f32[3,192,2048]{2,1,0:T(8,128)} %bitcast.74, bf16[3,2,192,1024]{3,2,1,0:T(8,128)(2,1)} %fusion.8.first, ...), custom_call_target="tpu_custom_call" | custom-call | flops 19327352832 | bytes 33554432 | tf_op jit(solution)/shard_map/pallas_call | solution.py:246
  479.0 4.3 fusion.61
  483.3 0.0 collective-permute-start.2
  483.3 0.5 collective-permute-start
  483.8 0.0 collective-permute-start.4
  483.8 2.9 fusion.60
  486.7 0.6 collective-permute-start.1
  487.3 0.1 collective-permute-start.3
  487.3 1.9 collective-permute-done.2
  489.3 0.1 collective-permute-start.5
  489.4 2.2 broadcast_select_fusion.7
  491.7 0.0 slice-start.1
  491.7 12.0 %fusion.1 = f32[768,2048]{1,0:T(8,128)} fusion(bf16[768,1024]{1,0:T(8,128)(2,1)S(1)} %get-tuple-element.22, bf16[768,1024]{1,0:T(8,128)(2,1)S(1)} %get-tuple-element.21, bf16[1,2048,2048]{2,1,0:T(8,128)(2,1)} %all-gather.5.cloned.1.call-done), kind=kOutput, calls=%fused_computation.31 | convolution fusion | flops 6448742400 | bytes 17825792 | tf_op jit(solution)/shard_map/dot_general | solution.py:308
  503.7 0.0 collective-permute-done
  503.7 0.3 broadcast_select_fusion.11
  504.0 8.8 %fusion.2 = f32[768,2048]{1,0:T(8,128)} fusion(bf16[768,1024]{1,0:T(8,128)(2,1)S(1)} %get-tuple-element.26, bf16[768,1024]{1,0:T(8,128)(2,1)S(1)} %get-tuple-element.25, bf16[1,2048,2048]{2,1,0:T(8,128)(2,1)S(1)} %bitcast.72), kind=kOutput, calls=%fused_computation.32 | convolution fusion | flops 6448742400 | bytes 17825792 | tf_op jit(solution)/shard_map/dot_general | solution.py:308
  512.9 0.0 collective-permute-done.1
  512.9 0.3 broadcast_select_fusion.9
  513.2 0.0 copy-start.12
  513.3 0.0 slice-start.3
  513.3 6.3 %fusion.3 = f32[2048,512]{1,0:T(8,128)S(1)} fusion(f32[768,2048]{1,0:T(8,128)} %fusion.2, s32[]{:T(128)S(6)} %select_n.72, bf16[768,1024]{1,0:T(8,128)(2,1)S(1)} %get-tuple-element.23, bf16[768,1024]{1,0:T(8,128)(2,1)S(1)} %get-tuple-element.24), kind=kOutput, calls=%fused_computation.33 | convolution fusion | flops 1620049920 | bytes 13631492 | tf_op jit(solution)/shard_map/dot_general | solution.py:22
  519.6 0.0 collective-permute-done.4
  519.6 0.3 broadcast_select_fusion.3
  520.0 0.0 collective-permute-done.3
  520.0 0.3 broadcast_select_fusion.5
  520.3 2.2 fusion.4
  522.6 0.0 collective-permute-done.5
  522.6 0.3 broadcast_select_fusion.1
  522.9 6.7 %fusion = f32[768,2048]{1,0:T(8,128)S(1)} fusion(bf16[768,1024]{1,0:T(8,128)(2,1)S(1)} %get-tuple-element.18, bf16[768,1024]{1,0:T(8,128)(2,1)S(1)} %get-tuple-element.17, bf16[1,2048,2048]{2,1,0:T(8,128)(2,1)S(1)} %bitcast.72), kind=kOutput, calls=%fused_computation.30 | convolution fusion | flops 6448742400 | bytes 17825792 | tf_op jit(solution)/shard_map/dot_general | solution.py:308
  529.7 2.6 copy-done.19
  532.3 3.5 fusion.7
  535.8 15.0 %fusion.9 = f32[512,2048]{1,0:T(8,128)} fusion(f32[768,2048]{1,0:T(8,128)} %fusion.2, bf16[768,1024]{1,0:T(8,128)(2,1)} %copy-done.12, bf16[768,1024]{1,0:T(8,128)(2,1)} %copy-done.11, s32[]{:T(128)S(6)} %select_n.72, bf16[768,1024]{1,0:T(8,128)(2,1)} %copy-done.7, bf16[768,1024]{1,0:T(8,128)(2,1)} %copy-done.8, ...), kind=kOutput, calls=%fused_computation.53 | convolution fusion | flops 8075083776 | bytes 25165828 | tf_op jit(solution)/shard_map/dot_general | solution.py:22
  550.9 14.7 %fusion.10 = f32[512,2048]{1,0:T(8,128)} fusion(f32[768,2048]{1,0:T(8,128)} %fusion.1, bf16[768,1024]{1,0:T(8,128)(2,1)} %copy-done.14, bf16[768,1024]{1,0:T(8,128)(2,1)} %copy-done.13, s32[]{:T(128)S(6)} %select_n.72, bf16[768,1024]{1,0:T(8,128)(2,1)S(1)} %copy-done.4, bf16[768,1024]{1,0:T(8,128)(2,1)S(1)} %copy-done.6, ...), kind=kOutput, calls=%fused_computation.54 | convolution fusion | flops 8075083776 | bytes 25165828 | tf_op jit(solution)/shard_map/dot_general | solution.py:22
  565.6 15.6 %fusion.6 = bf16[1,512,2048]{2,1,0:T(8,128)(2,1)} fusion(f32[512,2048]{1,0:T(8,128)} %fusion.9, f32[512,2048]{1,0:T(8,128)} %fusion.10, f32[768,2048]{1,0:T(8,128)} %copy-done.19, bf16[768,1024]{1,0:T(8,128)(2,1)} %copy-done.16, bf16[768,1024]{1,0:T(8,128)(2,1)} %copy-done.15, s32[]{:T(128)S(6)} %select_n.72, bf16[768,1024]{1,0:T(8,128)(2,1)} %copy-done.9, ...), kind=kOutput, calls=%fused_computation.36 | convolution fusion | flops 8078229504 | bytes 31457284 | tf_op jit(solution)/shard_map/dot_general | solution.py:22
  581.2 1.0 copy.12
  (43 shorter events, 0.1 us)
Async XLA Ops:
  7.2 1.7 copy-start
  7.2 2.8 copy-start.18
  7.2 154.8 %all-gather.5.cloned.1.call-start = ((), (), s32[]{:S(2)}) async-start(), calls=%async_computation | async-start | bytes 10485760 | tf_op jit(solution)/shard_map/all_gather | solution.py:285
  7.9 303.5 %all-gather.7.cloned.1.call-start = ((), (), s32[]{:S(2)}) async-start(), calls=%async_computation.1 | async-start | bytes 10485760 | tf_op jit(solution)/shard_map/all_gather | solution.py:286
  8.8 2.1 copy-start.2
  483.3 6.0 %collective-permute-start.2 = (bf16[768,1024]{1,0:T(8,128)(2,1)}, bf16[768,1024]{1,0:T(8,128)(2,1)}, u32[]{:S(2)}, u32[]{:S(2)}) collective-permute-start(bf16[768,1024]{1,0:T(8,128)(2,1)} %bitcast.12), channel_id=1, source_target_pairs={{0,1},{1,0},{2,3},{3,2},{4,5},{5,4},{6,7},{7,6},{8,9},{9,8},{10,11... | collective-permute-start | bytes 4718600 | tf_op jit(solution)/shard_map/ppermute | solution.py:18
  483.3 20.4 %collective-permute-start = (bf16[768,1024]{1,0:T(8,128)(2,1)S(1)}, bf16[768,1024]{1,0:T(8,128)(2,1)S(1)}, u32[]{:S(2)}, u32[]{:S(2)}) collective-permute-start(bf16[768,1024]{1,0:T(8,128)(2,1)S(1)} %bitcast.61), channel_id=1, source_target_pairs={{0,1},{1,0},{2,3},{3,2},{4,5},{5,4},{6,7},{7,6},{8,9},{9,8},{10,11... | collective-permute-start | bytes 4718600 | tf_op jit(solution)/shard_map/ppermute | solution.py:18
  483.8 35.8 %collective-permute-start.4 = (bf16[768,1024]{1,0:T(8,128)(2,1)S(1)}, bf16[768,1024]{1,0:T(8,128)(2,1)S(1)}, u32[]{:S(2)}, u32[]{:S(2)}) collective-permute-start(bf16[768,1024]{1,0:T(8,128)(2,1)S(1)} %bitcast.60), channel_id=1, source_target_pairs={{0,1},{1,0},{2,3},{3,2},{4,5},{5,4},{6,7},{7,6},{8,9},{9,8},{10,11... | collective-permute-start | bytes 4718600 | tf_op jit(solution)/shard_map/ppermute | solution.py:18
  486.7 26.2 %collective-permute-start.1 = (bf16[768,1024]{1,0:T(8,128)(2,1)S(1)}, bf16[768,1024]{1,0:T(8,128)(2,1)S(1)}, u32[]{:S(2)}, u32[]{:S(2)}) collective-permute-start(bf16[768,1024]{1,0:T(8,128)(2,1)S(1)} %bitcast.64), channel_id=1, source_target_pairs={{0,1},{1,0},{2,3},{3,2},{4,5},{5,4},{6,7},{7,6},{8,9},{9,8},{10,11... | collective-permute-start | bytes 4718600 | tf_op jit(solution)/shard_map/ppermute | solution.py:18
  487.3 32.7 %collective-permute-start.3 = (bf16[768,1024]{1,0:T(8,128)(2,1)S(1)}, bf16[768,1024]{1,0:T(8,128)(2,1)S(1)}, u32[]{:S(2)}, u32[]{:S(2)}) collective-permute-start(bf16[768,1024]{1,0:T(8,128)(2,1)S(1)} %bitcast.63), channel_id=1, source_target_pairs={{0,1},{1,0},{2,3},{3,2},{4,5},{5,4},{6,7},{7,6},{8,9},{9,8},{10,11... | collective-permute-start | bytes 4718600 | tf_op jit(solution)/shard_map/ppermute | solution.py:18
  489.3 33.3 %collective-permute-start.5 = (bf16[768,1024]{1,0:T(8,128)(2,1)S(1)}, bf16[768,1024]{1,0:T(8,128)(2,1)S(1)}, u32[]{:S(2)}, u32[]{:S(2)}) collective-permute-start(bf16[768,1024]{1,0:T(8,128)(2,1)S(1)} %bitcast.62), channel_id=1, source_target_pairs={{0,1},{1,0},{2,3},{3,2},{4,5},{5,4},{6,7},{7,6},{8,9},{9,8},{10,11... | collective-permute-start | bytes 4718600 | tf_op jit(solution)/shard_map/ppermute | solution.py:18
  489.4 14.6 %slice-start = ((s8[8388608]{0:T(1024)(128)(4,1)}), s8[4194304]{0:T(1024)(128)(4,1)S(1)}, s32[]{:S(2)}) async-start(s8[8388608]{0:T(1024)(128)(4,1)} %bitcast.71), calls=%async_computation.2 | async-start | bytes 8388608
  491.7 12.0 %copy-start.3 = (bf16[768,1024]{1,0:T(8,128)(2,1)}, bf16[768,1024]{1,0:T(8,128)(2,1)S(1)}, u32[]{:S(2)}) copy-start(bf16[768,1024]{1,0:T(8,128)(2,1)S(1)} %get-tuple-element.21) | copy-start | bytes 4718596
  491.7 12.0 %copy-start.5 = (bf16[768,1024]{1,0:T(8,128)(2,1)}, bf16[768,1024]{1,0:T(8,128)(2,1)S(1)}, u32[]{:S(2)}) copy-start(bf16[768,1024]{1,0:T(8,128)(2,1)S(1)} %get-tuple-element.22) | copy-start | bytes 4718596
  491.7 12.3 %slice-start.1 = ((s8[8388608]{0:T(1024)(128)(4,1)}), s8[4194304]{0:T(1024)(128)(4,1)S(1)}, s32[]{:S(2)}) async-start(s8[8388608]{0:T(1024)(128)(4,1)} %bitcast.71), calls=%async_computation.3 | async-start | bytes 8388608
  504.0 8.9 %copy-start.7 = (bf16[768,1024]{1,0:T(8,128)(2,1)}, bf16[768,1024]{1,0:T(8,128)(2,1)S(1)}, u32[]{:S(2)}) copy-start(bf16[768,1024]{1,0:T(8,128)(2,1)S(1)} %get-tuple-element.25) | copy-start | bytes 4718596
  504.0 8.9 %copy-start.8 = (bf16[768,1024]{1,0:T(8,128)(2,1)}, bf16[768,1024]{1,0:T(8,128)(2,1)S(1)}, u32[]{:S(2)}) copy-start(bf16[768,1024]{1,0:T(8,128)(2,1)S(1)} %get-tuple-element.26) | copy-start | bytes 4718596
  512.9 7.4 %slice-start.2 = ((s8[6291456]{0:T(1024)(128)(4,1)}), s8[4194304]{0:T(1024)(128)(4,1)S(1)}, s32[]{:S(2)}) async-start(s8[6291456]{0:T(1024)(128)(4,1)} %bitcast.75), calls=%async_computation.4 | async-start | bytes 8388608
  513.2 6.4 %copy-start.11 = (bf16[768,1024]{1,0:T(8,128)(2,1)}, bf16[768,1024]{1,0:T(8,128)(2,1)S(1)}, u32[]{:S(2)}) copy-start(bf16[768,1024]{1,0:T(8,128)(2,1)S(1)} %get-tuple-element.23) | copy-start | bytes 4718596
  513.2 6.4 %copy-start.12 = (bf16[768,1024]{1,0:T(8,128)(2,1)}, bf16[768,1024]{1,0:T(8,128)(2,1)S(1)}, u32[]{:S(2)}) copy-start(bf16[768,1024]{1,0:T(8,128)(2,1)S(1)} %get-tuple-element.24) | copy-start | bytes 4718596
  513.3 7.1 %slice-start.3 = ((s8[6291456]{0:T(1024)(128)(4,1)}), s8[2097152]{0:T(1024)(128)(4,1)S(1)}, s32[]{:S(2)}) async-start(s8[6291456]{0:T(1024)(128)(4,1)} %bitcast.75), calls=%async_computation.5 | async-start | bytes 4194304
  519.9 3.0 copy-start.9
  519.9 3.0 copy-start.10
  520.3 2.3 copy-start.13
  520.3 2.3 copy-start.14
  522.9 6.8 %copy-start.15 = (bf16[768,1024]{1,0:T(8,128)(2,1)}, bf16[768,1024]{1,0:T(8,128)(2,1)S(1)}, u32[]{:S(2)}) copy-start(bf16[768,1024]{1,0:T(8,128)(2,1)S(1)} %get-tuple-element.15) | copy-start | bytes 4718596
  522.9 6.8 %copy-start.16 = (bf16[768,1024]{1,0:T(8,128)(2,1)}, bf16[768,1024]{1,0:T(8,128)(2,1)S(1)}, u32[]{:S(2)}) copy-start(bf16[768,1024]{1,0:T(8,128)(2,1)S(1)} %get-tuple-element.16) | copy-start | bytes 4718596
  529.6 2.7 copy-start.19
  535.8 15.0 %copy-start.4 = (bf16[768,1024]{1,0:T(8,128)(2,1)S(1)}, bf16[768,1024]{1,0:T(8,128)(2,1)}, u32[]{:S(2)}) copy-start(bf16[768,1024]{1,0:T(8,128)(2,1)} %copy-done.3) | copy-start | bytes 4718596
  535.8 15.0 %copy-start.6 = (bf16[768,1024]{1,0:T(8,128)(2,1)S(1)}, bf16[768,1024]{1,0:T(8,128)(2,1)}, u32[]{:S(2)}) copy-start(bf16[768,1024]{1,0:T(8,128)(2,1)} %copy-done.5) | copy-start | bytes 4718596
  565.6 15.6 %copy-start.17 = (bf16[3,192,1024]{2,1,0:T(8,128)(2,1)S(1)}, bf16[3,192,1024]{2,1,0:T(8,128)(2,1)}, u32[]{:S(2)}) copy-start(bf16[3,192,1024]{2,1,0:T(8,128)(2,1)} %get-tuple-element.6) | copy-start | bytes 3538948
  565.6 16.6 %copy-start.1 = (bf16[1,3,192,2048]{3,2,1,0:T(8,128)(2,1)S(1)}, bf16[1,3,192,2048]{3,2,1,0:T(8,128)(2,1)}, u32[]{:S(2)}) copy-start(bf16[1,3,192,2048]{3,2,1,0:T(8,128)(2,1)} %param.5) | copy-start | bytes 7077892
Sparse Core Ops, SparseCore 0:
  9.6 152.3 all-gather.4
  163.5 147.8 all-gather.6

commit v3 on v2

v3 whole, which is shorter than its diff:
```python
import functools

import jax
import jax.numpy as jnp
from jax import lax
from jax.experimental import pallas as pl
from jax.experimental.pallas import tpu as pltpu
from jax.sharding import PartitionSpec as P


def slope(pre):
    sigma = jax.nn.sigmoid(pre)
    return sigma * (1.0 + pre * (1.0 - sigma))


MESH = pl.DeviceIdType.MESH
TILE = 512
UNIT = 256


def chain_kernel(
    sections, replicas, w_in, w_out, slopes, first, own_x,
    grads, dw_in, dw_out, all_x, all_g,
    g_buf, dpre, mine, give, take, x_now, g_now, x_turned, sum_in, sum_out,
    hop_send, hop_recv, fwd_send, fwd_recv, swap_send, swap_recv,
    x_send, x_recv, x_give, x_take, g_send, g_recv, g_give, g_take, load_sem,
):
    section = lax.axis_index("section")
    place = lax.axis_index("dp")
    core = lax.axis_index("mp")
    micros, _, rows, half = g_buf.shape
    hidden = dpre.shape[1]
    part = dw_in.shape[0]
    last = sections - 1

    barrier = pltpu.get_barrier_semaphore()
    greeted = [{"mp": 1 - core}]
    greeted += [{"dp": lax.rem(place + step, replicas)} for step in (1, replicas - 1)]
    greeted += [{"section": lax.rem(section + step, sections)} for step in (1, sections - 1)]
    for device in greeted:
        pl.semaphore_signal(barrier, inc=1, device_id=device, device_id_type=MESH)
    pl.semaphore_wait(barrier, len(greeted))

    def remote(src, dst, send, recv, device):
        return pltpu.make_async_remote_copy(
            src_ref=src, dst_ref=dst, send_sem=send, recv_sem=recv,
            device_id=device, device_id_type=MESH,
        )

    def sent(way, k):
        sign = 1 - 2 * way
        origin, to = place - sign * (k - 1), place + sign
        ok = (origin >= 0) & (origin < replicas) & (to >= 0) & (to < replicas)
        return jnp.clip(origin, 0, replicas - 1), jnp.clip(to, 0, replicas - 1), ok

    def came(way, k):
        origin = place - (1 - 2 * way) * k
        return jnp.clip(origin, 0, replicas - 1), (origin >= 0) & (origin < replicas)

    def own_stage(k):
        return isinstance(k, int) and k == 1

    def x_copy(way, k, origin, to):
        there = all_x.at[origin, core]
        src = own_x.at[core] if own_stage(k) else there
        return remote(src, there, x_send.at[way, k - 1], x_recv.at[way, k - 1], {"dp": to})

    def g_copy(way, k, m, origin, to):
        there = all_g.at[origin, core, pl.ds(m * rows, rows)]
        src = g_buf.at[m, core] if own_stage(k) else there
        return remote(
            src, there, g_send.at[way, k - 1, m], g_recv.at[way, k - 1, m], {"dp": to}
        )

    def x_share(way, k, origin, which):
        block = all_x.at[origin, which]
        return remote(
            block, block, x_give.at[way, k - 1], x_take.at[way, k - 1], {"mp": 1 - core}
        )

    def g_share(way, k, m, origin, which):
        block = all_g.at[origin, which, pl.ds(m * rows, rows)]
        return remote(
            block, block, g_give.at[way, k - 1, m], g_take.at[way, k - 1, m], {"mp": 1 - core}
        )

    def start(copy_of, k, *m):
        for way in range(2):
            origin, to, ok = sent(way, k)

            @pl.when(ok)
            def _():
                copy_of(way, k, *m, origin, to).start()

    def landed(copy_of, share_of, k, *m):
        for way in range(2):
            origin, ok = came(way, k)

            @pl.when(ok)
            def _():
                copy_of(way, k, *m, origin, origin).wait_recv()
                share_of(way, k, *m, origin, core).start()

    def left(copy_of, share_of, k, *m):
        for way in range(2):
            origin, to, ok = sent(way, k)

            @pl.when(ok)
            def _():
                copy_of(way, k, *m, origin, to).wait_send()

            source, here = came(way, k)

            @pl.when(here)
            def _():
                share_of(way, k, *m, source, core).wait_send()

    def hop(m):
        return remote(
            grads.at[m], g_buf.at[m, core], hop_send.at[m], hop_recv.at[m],
            {"section": jnp.maximum(section - 1, 0)},
        )

    def forward(m, which):
        return remote(
            g_buf.at[m, which], g_buf.at[m, which], fwd_send.at[m], fwd_recv.at[m],
            {"mp": 1 - core},
        )

    def swap(m):
        return remote(
            give.at[m], take.at[m], swap_send.at[m], swap_recv.at[m], {"mp": 1 - core}
        )

    def nt(left_block, right_block):
        return lax.dot_general(
            left_block, right_block, (((1,), (1,)), ((), ())),
            preferred_element_type=jnp.float32,
        )

    def nn(left_block, right_block):
        return jnp.dot(left_block, right_block, preferred_element_type=jnp.float32)

    start(x_copy, 1)
    sum_in[...] = jnp.zeros_like(sum_in)
    sum_out[...] = jnp.zeros_like(sum_out)
    for k in range(2, replicas):

        @pl.when(section <= last - k)
        def _():
            landed(x_copy, x_share, k - 1)
            start(x_copy, k)

    for m in range(micros):

        @pl.when(section == last)
        def _():
            g_buf[m] = first[m]

        @pl.when(section < last)
        def _():
            hop(m).wait_recv()
            forward(m, core).start()

        start(g_copy, 1, m)

        @pl.when(section < last)
        def _():
            forward(m, 1 - core).wait_recv()

        @pl.loop(0, hidden // TILE)
        def _(j):
            at = pl.ds(pl.multiple_of(j * TILE, TILE), TILE)
            total = nt(g_buf[m, 0], w_out[at, :half]) + nt(g_buf[m, 1], w_out[at, half:])
            dpre[:, at] = (total * slopes[m, :, at]).astype(jnp.bfloat16)

        @pl.loop(0, half // TILE)
        def _(j):
            at = pl.ds(pl.multiple_of(j * TILE, TILE), TILE)
            there = pl.ds(pl.multiple_of((1 - core) * half + j * TILE, TILE), TILE)
            give[m, :, at] = nt(dpre[...], w_in[there, :]).astype(jnp.bfloat16)

        swap(m).start()

        @pl.loop(0, half // TILE)
        def _(j):
            at = pl.ds(pl.multiple_of(j * TILE, TILE), TILE)
            here = pl.ds(pl.multiple_of(core * half + j * TILE, TILE), TILE)
            mine[:, at] = nt(dpre[...], w_in[here, :])

        swap(m).wait_recv()
        grads[m] = (
            g_buf[m, core].astype(jnp.float32) + (mine[...] + take[m].astype(jnp.float32))
        ).astype(jnp.bfloat16)

        @pl.when(section > 0)
        def _():
            hop(m).start()

    for k in range(2, replicas):

        @pl.when(section > last - k)
        def _():
            landed(x_copy, x_share, k - 1)
            start(x_copy, k)

    def weight_terms():
        column = place * part
        side = column // half
        span = pl.ds(pl.multiple_of(lax.rem(column, half), part), part)
        x_turned[...] = x_now[side, :, span].T

        @pl.loop(0, hidden // UNIT)
        def _(j):
            at = pl.ds(pl.multiple_of(j * UNIT, UNIT), UNIT)
            pre = nn(x_now[0], w_in[:half, at]) + nn(x_now[1], w_in[half:, at])
            sigma = jax.nn.sigmoid(pre)
            act = (pre * sigma).astype(jnp.bfloat16)
            total = nt(g_now[0], w_out[at, :half]) + nt(g_now[1], w_out[at, half:])
            slope_now = sigma * (1.0 + pre * (1.0 - sigma))
            dpre_now = (total * slope_now).astype(jnp.bfloat16)
            sum_in[:, at] += nn(x_turned[...], dpre_now)
            sum_out[at, :] += nn(act.T, g_now[side, :, span])

    @pl.loop(0, replicas)
    def _(k):
        @pl.when(k + 1 < replicas)
        def _():
            for m in range(micros):
                landed(g_copy, g_share, k + 1, m)

                @pl.when(k + 2 < replicas)
                def _():
                    start(g_copy, k + 2, m)

        @pl.when(k + 2 == replicas)
        def _():
            landed(x_copy, x_share, replicas - 1)

        @pl.loop(0, 2)
        def _(way):
            origin, there = came(way, k)

            @pl.when(there & ((k > 0) | (way == 0)))
            def _():
                @pl.when(k == 0)
                def _():
                    load = pltpu.make_async_copy(own_x, x_now, load_sem.at[0])
                    load.start()
                    for m in range(micros):
                        for side in range(2):
                            g_now[side, m * rows : (m + 1) * rows] = g_buf[m, side]
                    load.wait()

                @pl.when(k > 0)
                def _():
                    x_share(way, k, origin, 1 - core).wait_recv()
                    load = pltpu.make_async_copy(all_x.at[origin], x_now, load_sem.at[0])
                    load.start()
                    for m in range(micros):
                        g_share(way, k, m, origin, 1 - core).wait_recv()
                    load_g = pltpu.make_async_copy(all_g.at[origin], g_now, load_sem.at[1])
                    load_g.start()
                    load.wait()
                    load_g.wait()

                weight_terms()

    dw_in[...] = sum_in[...].astype(jnp.bfloat16)
    dw_out[...] = sum_out[...].astype(jnp.bfloat16)
    for m in range(micros):
        swap(m).wait_send()

        @pl.when(section < last)
        def _():
            forward(m, core).wait_send()

        @pl.when(section > 0)
        def _():
            hop(m).wait_send()

    for k in range(1, replicas):
        left(x_copy, x_share, k)
        for m in range(micros):
            left(g_copy, g_share, k, m)


def chain(sections, replicas, full_in, full_out, slopes, first, own_x):
    micros, cores, rows, half = first.shape
    hidden = full_out.shape[0]
    part = cores * half // replicas
    tokens = micros * rows
    vmem, hbm = pl.BlockSpec(memory_space=pltpu.VMEM), pl.BlockSpec(memory_space=pl.ANY)
    dma = pltpu.SemaphoreType.DMA
    everyone = jax.ShapeDtypeStruct((replicas, cores, tokens, half), jnp.bfloat16)
    block = (micros, rows, half)
    return pl.pallas_call(
        functools.partial(chain_kernel, sections, replicas),
        out_shape=(
            jax.ShapeDtypeStruct(block, jnp.bfloat16),
            jax.ShapeDtypeStruct((part, hidden), jnp.bfloat16),
            jax.ShapeDtypeStruct((hidden, part), jnp.bfloat16),
            everyone,
            everyone,
        ),
        in_specs=[vmem, vmem, vmem, vmem, hbm],
        out_specs=(vmem, vmem, vmem, hbm, hbm),
        scratch_shapes=[
            pltpu.VMEM(first.shape, jnp.bfloat16),
            pltpu.VMEM((rows, hidden), jnp.bfloat16),
            pltpu.VMEM((rows, half), jnp.float32),
            pltpu.VMEM(block, jnp.bfloat16),
            pltpu.VMEM(block, jnp.bfloat16),
            pltpu.VMEM((cores, tokens, half), jnp.bfloat16),
            pltpu.VMEM((cores, tokens, half), jnp.bfloat16),
            pltpu.VMEM((part, tokens), jnp.bfloat16),
            pltpu.VMEM((part, hidden), jnp.float32),
            pltpu.VMEM((hidden, part), jnp.float32),
        ]
        + [dma((micros,))] * 6
        + [dma((2, replicas - 1))] * 4
        + [dma((2, replicas - 1, micros))] * 4
        + [dma((2,))],
        compiler_params=pltpu.CompilerParams(
            collective_id=0, has_side_effects=True, vmem_limit_bytes=60 * 1024 * 1024
        ),
        cost_estimate=pl.CostEstimate(
            flops=8 * micros * rows * half * hidden * cores,
            bytes_accessed=8 * full_in.size,
            transcendentals=0,
        ),
    )(full_in, full_out, slopes, first, own_x)


def local(activations, out_grad, weight_in, weight_out, lengths):
    sections = lax.axis_size("section")
    mp_count = lax.axis_size("mp")
    dp_count = lax.axis_size("dp")
    micro_count, row_count, width = out_grad.shape
    half = width // mp_count
    hidden = weight_in.shape[2]
    saved = activations[0]
    full_in = lax.all_gather(weight_in[0], "dp", axis=0, tiled=True)
    full_out = lax.all_gather(weight_out[0], "dp", axis=1, tiled=True)
    valid = jnp.arange(row_count)[None, :] < lengths
    own_saved = saved.reshape(-1, mp_count, half).transpose(1, 0, 2)
    pre = jnp.dot(saved.reshape(-1, width), full_in, preferred_element_type=jnp.float32)
    slopes = slope(pre).reshape(micro_count, row_count, hidden)

    first = out_grad.reshape(micro_count, row_count, mp_count, half)
    first = jnp.where(valid[..., None, None], first, jnp.zeros_like(first)).transpose(0, 2, 1, 3)
    grads, dw_in, dw_out, _, _ = chain(
        sections, dp_count, full_in, full_out, slopes, first, own_saved
    )
    return grads[None], dw_in[None], dw_out[None]


def solution(mesh):
    return jax.shard_map(
        local,
        mesh=mesh,
        in_specs=(
            P("section", None, "dp", None),
            P(None, "dp", None),
            P("section", "dp", "mp"),
            P("section", "mp", "dp"),
            P(None, "dp"),
        ),
        out_specs=(
            P("section", None, "dp", "mp"),
            P("section", "dp", "mp"),
            P("section", "mp", "dp"),
        ),
        check_vma=False,
    )
```

time: 595 us -> 530 us (0.89)
  matrix products: 95.9 us -> 10.9 us
  Pallas kernels: 168 us -> 206 us
  waiting for transfers between devices: 291 us -> 284 us
    dot_general x9 -> x0, matrix products: 84.9 us -> none  [the longest x6 57.4 us: cross(): lax.dot_general(left, right, (((0,), (0,)), ((), ())), preferred_element_...]
    pallas_call x1, Pallas kernels: 168 us -> 206 us  [chain(): pl.pallas_call(functools.partial(chain_kernel, sections, replicas), out_s...]
    another operation x0 -> x2, local copies, waits for them, and re-layouts: none -> 7.71 us  [local(): own_saved = saved.reshape(-1, mp_count, half).transpose(1, 0, 2)]
    slice x2 -> x0, local copies, waits for them, and re-layouts: 7.16 us -> none  [the longest x1 4.29 us: local(): all_saved[i * chunk:(i + 1) * chunk]]
  transfers between devices with their start and end apart: 8 -> 2, of which waited for: 3 -> 2; matrix products, arithmetic and copies ran while one was open for 8% -> 4% of each run, Pallas kernels for 0% -> 0%
where the time goes in v3:
time: 530 us
  waiting for transfers between devices  284 us (54%)
  Pallas kernels  206 us (39%)
  between operations  14.1 us (3%)
  local copies, waits for them, and re-layouts  13.9 us (3%)
  matrix products  10.9 us (2%)
    pallas_call x1, Pallas kernels, chain(): pl.pallas_call(functools.partial(chain_kernel, sections, replicas), out_s...  206 us
    all_gather x1, waiting for transfers between devices, local(): full_in = lax.all_gather(weight_in[0], 'dp', axis=0, tiled=True)  144 us
    all_gather x1, waiting for transfers between devices, local(): full_out = lax.all_gather(weight_out[0], 'dp', axis=1, tiled=True)  139 us
    dot_general x1, matrix products, local(): jnp.dot(saved.reshape(-1, width), full_in, preferred_element_type=jnp.flo...  10.9 us
  transfers between devices with their start and end apart: 2, of which 2 were waited for; matrix products, arithmetic and copies ran while one was open for 4% of the time, Pallas kernels for 0%

profile of v3, /device:TPU:0, one launch (start us, length us, event | category | flops | bytes accessed | tf_op | source)
XLA Modules:
  0.0 530.0 jit_solution(730785865056821536)
XLA Ops:
  7.2 0.0 all-gather.5.cloned.1.call-start
  7.2 0.7 all-gather.5.cloned.1.call-update
  7.9 0.0 all-gather.7.cloned.1.call-start
  7.9 0.7 all-gather.7.cloned.1.call-update
  8.6 5.6 %reshape_squeeze.7 = bf16[576,2,1024]{2,1,0:T(2,128)(2,1)S(1)} reshape(bf16[1,3,192,2048]{3,2,1,0:T(8,128)(2,1)} %param.5) | data formatting | bytes 4718592 | tf_op jit(solution)/shard_map/reshape;squeeze | solution.py:346
  14.3 0.0 copy-start.4
  14.3 0.0 copy-start
  14.3 2.1 copy.13
  16.4 0.0 copy-done.4
  16.4 0.1 iota_compare_fusion
  16.5 0.0 copy-done
  16.5 0.0 copy-start.1
  16.5 1.7 fusion.first
  18.1 143.8 %all-gather.5.cloned.1.call-done = bf16[1,2048,2048]{2,1,0:T(8,128)(2,1)} async-done(((bf16[1,512,2048]{2,1,0:T(8,128)(2,1)}), bf16[1,2048,2048]{2,1,0:T(8,128)(2,1)}) %all-gather.5.cloned.1.call-update) | async-done | bytes 8388624 | tf_op jit(solution)/shard_map/all_gather | solution.py:343
  161.9 0.0 copy-done.1
  161.9 10.9 %add_multiply_fusion = f32[576,2048]{1,0:T(8,128)} fusion(bf16[576,2048]{1,0:T(8,128)(2,1)S(1)} %bitcast.26, bf16[1,2048,2048]{2,1,0:T(8,128)(2,1)} %all-gather.5.cloned.1.call-done), kind=kOutput, calls=%fused_computation | convolution fusion | flops 4840095744 | bytes 15466496 | tf_op jit(solution)/shard_map/dot_general | solution.py:347
  172.8 138.6 %all-gather.7.cloned.1.call-done = bf16[1,2048,2048]{2,1,0:T(8,128)(2,1)} async-done(((bf16[1,2048,512]{2,1,0:T(8,128)(2,1)}), bf16[1,2048,2048]{2,1,0:T(8,128)(2,1)}) %all-gather.7.cloned.1.call-update) | async-done | bytes 8388624 | tf_op jit(solution)/shard_map/all_gather | solution.py:344
  311.4 205.5 %shard_map.79 = (bf16[3,192,1024]{2,1,0:T(8,128)(2,1)}, bf16[512,2048]{1,0:T(8,128)(2,1)}, bf16[2048,512]{1,0:T(8,128)(2,1)}, bf16[4,2,576,1024]{3,2,1,0:T(8,128)(2,1)}, bf16[4,2,576,1024]{3,2,1,0:T(8,128)(2,1)}) custom-call(bf16[2048,2048]{1,0:T(8,128)(2,1)} %bitcast.31, bf16[2048,2048]{1,0:T(8,128)(2,1)} %bitcast.32, f32[3,192,2048]{2,1,0:T(8,128)} %bitcast.34, ...), custom_call_target="tpu_custom_call" | custom-call | flops 19327352832 | bytes 33554432 | tf_op jit(solution)/shard_map/pallas_call | solution.py:297
  516.9 0.0 copy-start.3
  516.9 2.5 copy.17
  519.5 0.0 copy-done.3
  519.5 0.0 copy-start.2
  519.5 1.3 copy.18
  520.8 1.0 copy-done.2
  521.8 1.3 copy.19
Async XLA Ops:
  7.2 154.8 %all-gather.5.cloned.1.call-start = ((), (), s32[]{:S(2)}) async-start(), calls=%async_computation | async-start | bytes 10485760 | tf_op jit(solution)/shard_map/all_gather | solution.py:343
  7.9 303.5 %all-gather.7.cloned.1.call-start = ((), (), s32[]{:S(2)}) async-start(), calls=%async_computation.1 | async-start | bytes 10485760 | tf_op jit(solution)/shard_map/all_gather | solution.py:344
  14.3 2.1 copy-start.4
  14.3 2.2 copy-start
  16.5 145.5 %copy-start.1 = (bf16[1,3,192,2048]{3,2,1,0:T(8,128)(2,1)S(1)}, bf16[1,3,192,2048]{3,2,1,0:T(8,128)(2,1)}, u32[]{:S(2)}) copy-start(bf16[1,3,192,2048]{3,2,1,0:T(8,128)(2,1)} %param.5) | copy-start | bytes 7077892
  516.9 2.5 copy-start.3
  519.5 2.3 copy-start.2
Sparse Core Ops, SparseCore 0:
  9.6 152.3 all-gather.4
  163.5 147.8 all-gather.6

commit v4 on v3

--- a/solution.py
+++ b/solution.py
@@ -19,10 +19,11 @@
 
 
 def chain_kernel(
-    sections, replicas, w_in, w_out, slopes, first, own_x,
+    sections, replicas, own_in, own_out, first, own_x,
     grads, dw_in, dw_out, all_x, all_g,
-    g_buf, dpre, mine, give, take, x_now, g_now, x_turned, sum_in, sum_out,
+    w_in, w_out, slopes, g_buf, dpre, mine, give, take, x_now, g_now, x_turned, sum_in, sum_out,
     hop_send, hop_recv, fwd_send, fwd_recv, swap_send, swap_recv,
+    in_send, in_recv, out_send, out_recv,
     x_send, x_recv, x_give, x_take, g_send, g_recv, g_give, g_take, load_sem,
 ):
     section = lax.axis_index("section")
@@ -60,6 +61,19 @@
     def own_stage(k):
         return isinstance(k, int) and k == 1
 
+    def block_of(origin):
+        return pl.ds(pl.multiple_of(origin * part, part), part)
+
+    def in_copy(way, k, origin, to):
+        there = w_in.at[block_of(origin)]
+        src = own_in if own_stage(k) else there
+        return remote(src, there, in_send.at[way, k - 1], in_recv.at[way, k - 1], {"dp": to})
+
+    def out_copy(way, k, origin, to):
+        there = w_out.at[:, block_of(origin)]
+        src = own_out if own_stage(k) else there
+        return remote(src, there, out_send.at[way, k - 1], out_recv.at[way, k - 1], {"dp": to})
+
     def x_copy(way, k, origin, to):
         there = all_x.at[origin, core]
         src = own_x.at[core] if own_stage(k) else there
@@ -99,7 +113,8 @@
             @pl.when(ok)
             def _():
                 copy_of(way, k, *m, origin, origin).wait_recv()
-                share_of(way, k, *m, origin, core).start()
+                if share_of is not None:
+                    share_of(way, k, *m, origin, core).start()
 
     def left(copy_of, share_of, k, *m):
         for way in range(2):
@@ -111,9 +126,11 @@
 
             source, here = came(way, k)
 
-            @pl.when(here)
-            def _():
-                share_of(way, k, *m, source, core).wait_send()
+            if share_of is not None:
+
+                @pl.when(here)
+                def _():
+                    share_of(way, k, *m, source, core).wait_send()
 
     def hop(m):
         return remote(
@@ -141,9 +158,49 @@
     def nn(left_block, right_block):
         return jnp.dot(left_block, right_block, preferred_element_type=jnp.float32)
 
-    start(x_copy, 1)
+    def pre_terms(origin, fresh):
+        column = origin * part
+        span = pl.ds(pl.multiple_of(lax.rem(column, half), part), part)
+
+        @pl.loop(0, hidden // TILE)
+        def _(j):
+            at = pl.ds(pl.multiple_of(j * TILE, TILE), TILE)
+            terms = nn(x_now[column // half, :, span], w_in[block_of(origin), at])
+            slopes[:, at] = terms if fresh else slopes[:, at] + terms
+
+    start(in_copy, 1)
+    start(out_copy, 1)
+    loads = [
+        pltpu.make_async_copy(own_in, w_in.at[block_of(place)], load_sem.at[0]),
+        pltpu.make_async_copy(own_x, x_now, load_sem.at[1]),
+        pltpu.make_async_copy(own_out, w_out.at[:, block_of(place)], load_sem.at[2]),
+    ]
+    for load in loads:
+        load.start()
+    for load in loads:
+        load.wait()
+    pre_terms(place, True)
     sum_in[...] = jnp.zeros_like(sum_in)
     sum_out[...] = jnp.zeros_like(sum_out)
+    for k in range(1, replicas):
+        for copy_of in (in_copy, out_copy):
+            landed(copy_of, None, k)
+            if k + 1 < replicas:
+                start(copy_of, k + 1)
+        if k == replicas - 2:
+            start(x_copy, 1)
+        for way in range(2):
+            origin, there = came(way, k)
+
+            @pl.when(there)
+            def _():
+                pre_terms(origin, False)
+
+    @pl.loop(0, hidden // TILE)
+    def _(j):
+        at = pl.ds(pl.multiple_of(j * TILE, TILE), TILE)
+        slopes[:, at] = slope(slopes[:, at])
+
     for k in range(2, replicas):
 
         @pl.when(section <= last - k)
@@ -172,7 +229,7 @@
         def _(j):
             at = pl.ds(pl.multiple_of(j * TILE, TILE), TILE)
             total = nt(g_buf[m, 0], w_out[at, :half]) + nt(g_buf[m, 1], w_out[at, half:])
-            dpre[:, at] = (total * slopes[m, :, at]).astype(jnp.bfloat16)
+            dpre[:, at] = (total * slopes[pl.ds(m * rows, rows), at]).astype(jnp.bfloat16)
 
         @pl.loop(0, half // TILE)
         def _(j):
@@ -245,12 +302,9 @@
             def _():
                 @pl.when(k == 0)
                 def _():
-                    load = pltpu.make_async_copy(own_x, x_now, load_sem.at[0])
-                    load.start()
                     for m in range(micros):
                         for side in range(2):
                             g_now[side, m * rows : (m + 1) * rows] = g_buf[m, side]
-                    load.wait()
 
                 @pl.when(k > 0)
                 def _():
@@ -280,15 +334,17 @@
             hop(m).wait_send()
 
     for k in range(1, replicas):
+        left(in_copy, None, k)
+        left(out_copy, None, k)
         left(x_copy, x_share, k)
         for m in range(micros):
             left(g_copy, g_share, k, m)
 
 
-def chain(sections, replicas, full_in, full_out, slopes, first, own_x):
+def chain(sections, replicas, own_in, own_out, first, own_x):
     micros, cores, rows, half = first.shape
-    hidden = full_out.shape[0]
-    part = cores * half // replicas
+    part, hidden = own_in.shape
+    width = cores * half
     tokens = micros * rows
     vmem, hbm = pl.BlockSpec(memory_space=pltpu.VMEM), pl.BlockSpec(memory_space=pl.ANY)
     dma = pltpu.SemaphoreType.DMA
@@ -303,9 +359,12 @@
             everyone,
             everyone,
         ),
-        in_specs=[vmem, vmem, vmem, vmem, hbm],
+        in_specs=[hbm, hbm, vmem, hbm],
         out_specs=(vmem, vmem, vmem, hbm, hbm),
         scratch_shapes=[
+            pltpu.VMEM((width, hidden), jnp.bfloat16),
+            pltpu.VMEM((hidden, width), jnp.bfloat16),
+            pltpu.VMEM((tokens, hidden), jnp.float32),
             pltpu.VMEM(first.shape, jnp.bfloat16),
             pltpu.VMEM((rows, hidden), jnp.bfloat16),
             pltpu.VMEM((rows, half), jnp.float32),
@@ -318,18 +377,18 @@
             pltpu.VMEM((hidden, part), jnp.float32),
         ]
         + [dma((micros,))] * 6
-        + [dma((2, replicas - 1))] * 4
+        + [dma((2, replicas - 1))] * 8
         + [dma((2, replicas - 1, micros))] * 4
-        + [dma((2,))],
+        + [dma((3,))],
         compiler_params=pltpu.CompilerParams(
             collective_id=0, has_side_effects=True, vmem_limit_bytes=60 * 1024 * 1024
         ),
         cost_estimate=pl.CostEstimate(
             flops=8 * micros * rows * half * hidden * cores,
-            bytes_accessed=8 * full_in.size,
+            bytes_accessed=8 * width * hidden,
             transcendentals=0,
         ),
-    )(full_in, full_out, slopes, first, own_x)
+    )(own_in, own_out, first, own_x)
 
 
 def local(activations, out_grad, weight_in, weight_out, lengths):
@@ -338,19 +397,13 @@
     dp_count = lax.axis_size("dp")
     micro_count, row_count, width = out_grad.shape
     half = width // mp_count
-    hidden = weight_in.shape[2]
     saved = activations[0]
-    full_in = lax.all_gather(weight_in[0], "dp", axis=0, tiled=True)
-    full_out = lax.all_gather(weight_out[0], "dp", axis=1, tiled=True)
     valid = jnp.arange(row_count)[None, :] < lengths
     own_saved = saved.reshape(-1, mp_count, half).transpose(1, 0, 2)
-    pre = jnp.dot(saved.reshape(-1, width), full_in, preferred_element_type=jnp.float32)
-    slopes = slope(pre).reshape(micro_count, row_count, hidden)
-
     first = out_grad.reshape(micro_count, row_count, mp_count, half)
     first = jnp.where(valid[..., None, None], first, jnp.zeros_like(first)).transpose(0, 2, 1, 3)
     grads, dw_in, dw_out, _, _ = chain(
-        sections, dp_count, full_in, full_out, slopes, first, own_saved
+        sections, dp_count, weight_in[0], weight_out[0], first, own_saved
     )
     return grads[None], dw_in[None], dw_out[None]
 

time: 530 us -> 488 us (0.921)
  waiting for transfers between devices: 284 us -> 0 us
  Pallas kernels: 206 us -> 470 us
  between operations: 14.1 us -> 0.66 us
  matrix products: 10.9 us -> 0 us
    all_gather x2 -> x0, waiting for transfers between devices: 282 us -> none  [the longest x1 144 us: local(): full_in = lax.all_gather(weight_in[0], 'dp', axis=0, tiled=True)]
    pallas_call x1, Pallas kernels: 206 us -> 470 us  [chain(): pl.pallas_call(functools.partial(chain_kernel, sections, replicas), out_s...]
    dot_general x1 -> x0, matrix products: 10.9 us -> none  [local(): jnp.dot(saved.reshape(-1, width), full_in, preferred_element_type=jnp.flo...]
  transfers between devices with their start and end apart: 2 -> 0, of which waited for: 2 -> 0; matrix products, arithmetic and copies ran while one was open for 4% -> 0% of each run, Pallas kernels for 0% -> 0%
where the time goes in v4:
time: 488 us
  Pallas kernels  470 us (96%)
  local copies, waits for them, and re-layouts  13.9 us (3%)
    pallas_call x1, Pallas kernels, chain(): pl.pallas_call(functools.partial(chain_kernel, sections, replicas), out_s...  470 us

profile of v4, /device:TPU:0, one launch (start us, length us, event | category | flops | bytes accessed | tf_op | source)
XLA Modules:
  0.0 488.2 jit_solution(6065375005807575251)
XLA Ops:
  0.6 0.7 iota_compare_fusion
  1.4 3.3 fusion.first
  4.7 5.6 %reshape_squeeze.3 = bf16[576,2,1024]{2,1,0:T(2,128)(2,1)S(1)} reshape(bf16[1,3,192,2048]{3,2,1,0:T(8,128)(2,1)} %param.5) | data formatting | bytes 4718592 | tf_op jit(solution)/shard_map/reshape;squeeze | solution.py:402
  10.2 2.2 copy.13
  12.4 469.5 %shard_map.79 = (bf16[3,192,1024]{2,1,0:T(8,128)(2,1)}, bf16[512,2048]{1,0:T(8,128)(2,1)}, bf16[2048,512]{1,0:T(8,128)(2,1)}, bf16[4,2,576,1024]{3,2,1,0:T(8,128)(2,1)}, bf16[4,2,576,1024]{3,2,1,0:T(8,128)(2,1)}) custom-call(bf16[512,2048]{1,0:T(8,128)(2,1)} %bitcast.23, bf16[2048,512]{1,0:T(8,128)(2,1)} %bitcast.24, bf16[3,2,192,1024]{3,2,1,0:T(8,128)(2,1)} %fusion.first, ...), custom_call_target="tpu_custom_call" | custom-call | flops 19327352832 | bytes 33554432 | tf_op jit(solution)/shard_map/pallas_call | solution.py:353
  482.0 0.0 copy-start.1
  482.0 2.5 copy.17
  484.5 0.0 copy-done.1
  484.5 0.0 copy-start
  484.5 1.3 copy.18
  485.8 1.0 copy-done
  486.8 1.3 copy.19
Async XLA Ops:
  482.0 2.5 copy-start.1
  484.5 2.3 copy-start
